TPU v7x, 512 devices: a whole 4x8x8 slice. The times are simulated.
512 devices in a mesh: sec: 2 (over core), seq: 32 (over y, x), mp: 8 (over z).
Axes of the slice: x: 4, y: 8, z: 8, core: 2. Of those that a mesh axis runs over, the one named last changes fastest.
Arguments:
- hidden: bfloat16 [2, 4608, 8192], P(None, 'seq'), may hold values from -6 to 6
- norm_gain: float32 [2, 8192], P('sec'), may hold values from 0.1 to 1.9
- query_weight: bfloat16 [2, 8192, 4096], P('sec', 'seq', 'mp'), may hold values from -0.0625 to 0.0625
- keyvalue_weight: bfloat16 [2, 8192, 2, 1024], P('sec', 'seq', None, 'mp'), may hold values from -0.0625 to 0.0625
- policy_head: float32 [4096], P('mp'), may hold values from -0.3125 to 0.3125
- critic_heads: float32 [2, 4096], P(None, 'mp'), may hold values from -0.3125 to 0.3125
- lengths: int32 [2, 64], replicated, may hold values from 1 to 576, 4608 in all within a row
Outputs:
- policy_scores: float32 [2, 4608], P(None, 'seq')
- advantages: float32 [2, 4608], P(None, 'seq')
- returns: float32 [2, 4608], P(None, 'seq')
Inputs may be any that keep to these rules, and one draw needn't show every extreme that they name: Each micro-batch's lengths sum to 4608; in each micro-batch one length is exactly 576.
All inputs are finite; a program needn't handle non-finite values.
Results may differ from a plain program's by a relative error of at most 0.0071.
Values may be sent and summed in bfloat16 or wider, within the bound.
A program may use at most 128 MiB of HBM per device.

v0:
```python
import jax
import jax.numpy as jnp
from jax import lax
from jax.sharding import PartitionSpec as P

HEAD_DIM = 128
REACH = 4


LAMBDA_GAE = 0.95
ROPE_BASE = 1000000.0
NORM_EPS = 1e-06


def shifted(block, axis, distance):
    devices = range(lax.axis_size(axis))
    route = [(i - distance, i) for i in devices if i - distance in devices]
    return lax.ppermute(block, axis, route)


def row_info(row_index, lengths_row, count_rows):
    closing = jnp.cumsum(lengths_row)
    opening_rows = closing - lengths_row
    response = jnp.sum((row_index[:, None] >= closing[None, :]).astype(jnp.int32), axis=1)
    response = jnp.where(row_index < 0, -1, response)
    opening = jnp.max(
        jnp.where(opening_rows[None, :] <= row_index[:, None], opening_rows[None, :], 0), axis=1
    )
    position = row_index - opening
    inside = (row_index >= 0) & (row_index < count_rows)
    finish = jnp.any(closing[None, :] == row_index[:, None] + 1, axis=1) & inside
    follows = inside & jnp.logical_not(finish)
    return (response, opening, position, finish, follows, inside)


def rotary_tables(position, head_size):
    half_size = head_size // 2
    counter = jnp.arange(half_size).astype(jnp.float32)
    inverse = jnp.exp(-jnp.log(jnp.float32(ROPE_BASE)) * (2.0 * counter / head_size))
    angles = position.astype(jnp.float32)[..., None] * inverse
    angles = jnp.concatenate([angles, angles], axis=-1)
    return (jnp.cos(angles), jnp.sin(angles))


def rotate(vectors, cosine, sine):
    half_size = vectors.shape[-1] // 2
    turned = jnp.concatenate([-vectors[..., half_size:], vectors[..., :half_size]], axis=-1)
    return vectors * cosine[..., None, :] + turned * sine[..., None, :]


def combine_maps(earlier, later):
    return (later[0] * earlier[0], later[0] * earlier[1] + later[1])


def advantage_terms(value, value_next, reward, finish, follows):
    delta = jnp.where(finish, reward, 0.0) + value_next - value
    decay = LAMBDA_GAE * follows.astype(jnp.float32)
    flipped = lax.associative_scan(
        combine_maps, (decay[..., ::-1], delta[..., ::-1]), axis=value.ndim - 1
    )
    return (flipped[0][..., ::-1], flipped[1][..., ::-1])


def project_piece(normed, piece):
    return jnp.dot(normed, piece.reshape(piece.shape[0], -1), preferred_element_type=jnp.float32)


def attend_single(operands):
    queries, keys, values, query_resp, key_resp, query_pos, key_pos = operands
    score_scale = float(HEAD_DIM) ** (-0.5)
    scores = (
        jnp.einsum("qkgd,skd->kgqs", queries, keys, preferred_element_type=jnp.float32)
        * score_scale
    )
    allowed = (query_resp[:, None] == key_resp[None, :]) & (key_pos[None, :] <= query_pos[:, None])
    weights = jnp.where(allowed[None, None], jnp.exp(scores), 0.0)
    probs = (weights / jnp.sum(weights, axis=-1, keepdims=True)).astype(jnp.bfloat16)
    attended = jnp.einsum("kgqs,skd->qkgd", probs, values, preferred_element_type=jnp.float32)
    return attended.reshape(attended.shape[0], -1)


def on_device(hidden, norm_gain, query_weight, keyvalue_weight, policy_head, critic_heads, lengths):
    micro_count, shard_rows, width = hidden.shape
    seq_count = lax.axis_size("seq")
    seq_place = lax.axis_index("seq")
    section_place = lax.axis_index("sec")
    query_cols = query_weight.shape[2]
    kv_cols = keyvalue_weight.shape[3]
    kv_local = kv_cols // HEAD_DIM
    group_size = query_cols // kv_cols
    token_count = shard_rows * seq_count
    flat_rows = hidden.reshape(micro_count * shard_rows, width).astype(jnp.float32)
    scale = lax.rsqrt(jnp.mean(flat_rows * flat_rows, axis=1, keepdims=True) + NORM_EPS)
    normed = (flat_rows * scale * norm_gain[0][None, :]).astype(jnp.bfloat16)

    def add_single(piece):
        return project_piece(normed, piece[0])

    queries = add_single(lax.all_gather(query_weight, "seq", axis=1, tiled=True))
    keyvalue = add_single(lax.all_gather(keyvalue_weight, "seq", axis=1, tiled=True))
    local_index = seq_place * shard_rows + jnp.arange(shard_rows, dtype=jnp.int32)
    local_info = jax.vmap(lambda lengths_row: row_info(local_index, lengths_row, token_count))(
        lengths
    )
    local_resp, local_open, local_pos, local_finish, local_follows, local_inside = local_info
    cosine, sine = rotary_tables(local_pos, HEAD_DIM)
    queries = rotate(
        queries.reshape(micro_count, shard_rows, query_cols // HEAD_DIM, HEAD_DIM), cosine, sine
    )
    queries = queries.astype(jnp.bfloat16).reshape(micro_count, shard_rows, query_cols)
    keys = rotate(
        keyvalue[:, :kv_cols].reshape(micro_count, shard_rows, kv_local, HEAD_DIM), cosine, sine
    )
    keys = keys.astype(jnp.bfloat16).reshape(micro_count, shard_rows, kv_cols)
    values = keyvalue[:, kv_cols:].astype(jnp.bfloat16).reshape(micro_count, shard_rows, kv_cols)
    packed = jnp.concatenate([queries, keys, values], axis=2)
    heads_table = jnp.stack([policy_head, critic_heads[0], critic_heads[1]], axis=1)
    actor_side = (section_place == 0).astype(jnp.float32)
    section_mask = jnp.stack([actor_side, 1.0 - actor_side, 1.0 - actor_side])
    heads_table = heads_table * section_mask[None, :]
    ahead = [shifted(packed, "seq", -offset) for offset in range(1, REACH + 1)]
    window = jnp.concatenate([packed] + ahead, axis=1)
    span_rows = window.shape[1]
    window_index = seq_place * shard_rows + jnp.arange(span_rows, dtype=jnp.int32)
    window_info = jax.vmap(lambda lengths_row: row_info(window_index, lengths_row, token_count))(
        lengths
    )
    response, opening, position, finish, follows, inside = window_info
    window_query = window[:, :, :query_cols].reshape(
        micro_count, span_rows, kv_local, group_size, HEAD_DIM
    )
    window_keys = window[:, :, query_cols : query_cols + kv_cols].reshape(
        micro_count, span_rows, kv_local, HEAD_DIM
    )
    window_values = window[:, :, query_cols + kv_cols :].reshape(
        micro_count, span_rows, kv_local, HEAD_DIM
    )
    window_pos = jnp.broadcast_to(window_index[None, :], (micro_count, span_rows))
    attended = lax.map(
        attend_single,
        (window_query, window_keys, window_values, response, response, window_pos, window_pos),
    )
    partial_sums = jnp.dot(attended, heads_table, precision=lax.Precision.HIGHEST)
    summed = lax.psum(partial_sums, ("sec", "mp"))
    policy = summed[..., 0]
    value = summed[..., 1]
    reward = summed[..., 2]
    value_next = jnp.concatenate([value[:, 1:], jnp.zeros((micro_count, 1), jnp.float32)], axis=1)
    value_next = value_next * follows.astype(jnp.float32)
    decay_sum, advantage = advantage_terms(value, value_next, reward, finish, follows)
    owned = (opening // shard_rows == seq_place) & inside
    results = jnp.stack([policy, advantage, advantage + value], axis=2) * owned[..., None].astype(
        jnp.float32
    )
    gathered_back = results[:, :shard_rows]
    for offset in range(1, REACH + 1):
        gathered_back = gathered_back + shifted(
            results[:, offset * shard_rows : (offset + 1) * shard_rows], "seq", offset
        )
    return (gathered_back[..., 0], gathered_back[..., 1], gathered_back[..., 2])


def solution(mesh):
    placed = (
        P(None, "seq", None),
        P("sec", None),
        P("sec", "seq", "mp"),
        P("sec", "seq", None, "mp"),
        P("mp"),
        P(None, "mp"),
        P(),
    )
    return jax.shard_map(
        on_device,
        mesh=mesh,
        in_specs=placed,
        out_specs=(P(None, "seq"), P(None, "seq"), P(None, "seq")),
        check_vma=False,
    )
```

profile of v0, /device:TPU:1, one launch (start us, length us, event | category | flops | bytes accessed | tf_op | source)
XLA Modules:
  0.0 391.0 jit_solution(17401936054619056442)
XLA Ops:
  7.2 0.7 all-gather.5.cloned.1.call-update
  8.0 0.7 all-gather.3.cloned.1.call-update
  8.7 0.9 reduce_window_sum.12
  9.6 0.7 sub.30
  10.6 3.5 fusion.15
  14.4 3.5 fusion.17
  17.9 83.3 %all-gather.5.cloned.1.call-done = bf16[1,8192,2,128]{3,2,0,1:T(2,128)(2,1)} async-done(((bf16[1,256,2,128]{3,2,0,1:T(2,128)(2,1)}), bf16[1,8192,2,128]{3,2,0,1:T(2,128)(2,1)}) %all-gather.5.cloned.1.call-update) | async-done | bytes 4194320 | tf_op jit(solution)/shard_map/all_gather | solution.py:100
  101.1 5.0 %fusion.20 = f32[288,256]{1,0:T(8,128)S(1)} fusion(bf16[288,8192]{1,0:T(8,128)(2,1)} %bitcast.144, bf16[1024,8,2,128]{3,2,1,0:T(2,128)(2,1)} %bitcast.165), kind=kOutput, calls=%fused_computation.28 | convolution fusion | flops 1207959552 | bytes 9207808 | tf_op jit(solution)/shard_map/dot_general | solution.py:65
  106.3 0.6 fusion.30
  107.0 100.6 %all-gather.3.cloned.1.call-done = bf16[1,8192,512]{2,1,0:T(8,128)(2,1)} async-done(((bf16[1,256,512]{2,1,0:T(8,128)(2,1)}), bf16[1,8192,512]{2,1,0:T(8,128)(2,1)}) %all-gather.3.cloned.1.call-update) | async-done | bytes 8388624 | tf_op jit(solution)/shard_map/all_gather | solution.py:99
  207.5 11.9 %copy.37 = bf16[512,8192]{1,0:T(8,128)(2,1)} copy(bf16[512,8192]{0,1:T(8,128)(2,1)} %bitcast.142) | data formatting | bytes 16777216 | tf_op jit(solution)/shard_map/dot_general | solution.py:65
  219.5 6.5 %fusion.18 = f32[2,144,4,128]{3,1,2,0:T(8,128)S(1)} fusion(bf16[4,128,8192,1]{2,1,0,3:T(8,128)(2,1)} %bitcast.143, bf16[2,144,8192]{2,1,0:T(8,128)(2,1)} %fusion.17), kind=kOutput, calls=%fused_computation.26 | convolution fusion | flops 2415919104 | bytes 13697024 | tf_op jit(solution)/shard_map/dot_general | solution.py:65
  226.3 0.2 copy_bitcast_fusion.2
  226.6 1.3 collective-permute-start
  227.9 1.3 collective-permute-start.1
  229.2 1.3 collective-permute-start.2
  230.7 1.5 collective-permute-start.3
  232.2 13.1 %collective-permute-done = bf16[2,144,768]{2,1,0:T(8,128)(2,1)S(1)} collective-permute-done((bf16[2,144,768]{2,1,0:T(8,128)(2,1)S(1)}, bf16[2,144,768]{2,1,0:T(8,128)(2,1)S(1)}, u32[]{:S(2)}, u32[]{:S(2)}) %collective-permute-start) | collective-permute-done | bytes 442400 | tf_op jit(solution)/shard_map/ppermute | solution.py:18
  245.3 6.1 %collective-permute-done.1 = bf16[2,144,768]{2,1,0:T(8,128)(2,1)S(1)} collective-permute-done((bf16[2,144,768]{2,1,0:T(8,128)(2,1)S(1)}, bf16[2,144,768]{2,1,0:T(8,128)(2,1)S(1)}, u32[]{:S(2)}, u32[]{:S(2)}) %collective-permute-start.1) | collective-permute-done | bytes 442400 | tf_op jit(solution)/shard_map/ppermute | solution.py:18
  251.5 24.7 %collective-permute-done.3 = bf16[2,144,768]{2,1,0:T(8,128)(2,1)S(1)} collective-permute-done((bf16[2,144,768]{2,1,0:T(8,128)(2,1)S(1)}, bf16[2,144,768]{2,1,0:T(8,128)(2,1)S(1)}, u32[]{:S(2)}, u32[]{:S(2)}) %collective-permute-start.3) | collective-permute-done | bytes 442400 | tf_op jit(solution)/shard_map/ppermute | solution.py:18
  276.3 1.4 copy-done.1
  277.7 0.9 slice_bitcast_fusion
  278.6 1.5 slice.386
  280.0 0.4 reshape.280
  280.4 17.2 %while.10 = (s32[]{:T(128)}, f32[2,720,512]{2,1,0:T(8,128)}, bf16[2,720,1,128]{3,1,2,0:T(8,128)(2,1)}, s32[2,720]{1,0:T(2,128)S(1)}, s32[2,720]{1,0:T(2,128)S(1)...) while((s32[]{:T(128)}, f32[2,720,512]{2,1,0:T(8,128)}, ...), condition=%wide.region_6.7_spmd, body=%wide.region_4.6_spmd.sunk | while | flops 1077750784 | bytes 53828164 | solution.py:139
  280.5 0.5 compare_and_fusion.2
  281.0 0.3 constant_dynamic-slice_fusion.2
  281.3 2.5 fusion.73
  283.8 2.9 fusion.74
  286.6 0.6 copy.100
  287.4 1.6 copy-done.3
  289.1 0.5 compare_and_fusion.2
  289.6 0.3 constant_dynamic-slice_fusion.2
  289.8 2.5 fusion.73
  292.3 2.9 fusion.74
  295.2 0.6 copy.100
  296.0 1.6 copy-done.3
  297.6 4.4 %fusion.32 = f32[2,720,3]{1,2,0:T(4,128)S(1)} fusion(f32[2,720,512]{2,1,0:T(8,128)} %get-tuple-element.40, f32[512,1]{0,1:T(1,128)S(1)} %get-tuple-element.116, f32[512,1]{0,1:T(1,128)S(1)} %get-tuple-element.115, f32[512,1]{0,1:T(1,128)S(1)} %bitcast.164, f32[3]{0:T(128)S(1)} %pad_maximum_fusion.10), kind=kOutput, calls=%fused_computation.66 | convolution fusion | flops 26546688 | bytes 2972556 | tf_op jit(solution)/shard_map/dot_general | solution.py:143
  302.0 56.0 %psum.7 = f32[2,720,3]{1,2,0:T(4,128)S(1)} all-reduce(f32[2,720,3]{1,2,0:T(4,128)S(1)} %fusion.32), channel_id=1, replica_groups=mesh['sec'=2,'seq'=32,'mp'=8] {'sec','mp'}, use_global_device_ids=true, to_apply=%region_7.8 | all-reduce | flops 4320 | bytes 34560 | tf_op jit(solution)/shard_map/psum | solution.py:144
  358.3 0.2 slice.303
  358.6 0.2 slice.301
  358.8 0.3 reverse.12
  359.1 0.3 reverse.10
  359.4 0.2 slice.317
  359.6 0.2 slice.313
  359.9 0.2 slice.312
  360.2 0.2 slice.368
  360.4 0.2 slice.307
  360.6 0.2 slice.305
  360.9 0.3 reverse.11
  361.1 0.3 reverse.9
  361.5 0.2 slice.366
  361.9 0.2 slice.314
  366.6 0.3 reverse.8
  366.9 0.3 reverse.7
  369.9 0.2 pad.72
  370.2 0.2 pad.73
  370.4 0.5 reverse.13
  371.2 1.3 collective-permute-start.4
  372.5 2.4 collective-permute-start.7
  374.8 6.6 %collective-permute-start.6 = (f32[2,144,3]{1,0,2:T(2,128)S(1)}, f32[2,144,3]{1,0,2:T(2,128)S(1)}, u32[]{:S(2)}, u32[]{:S(2)}) collective-permute-start(f32[2,144,3]{1,0,2:T(2,128)S(1)} %get-tuple-element.108), channel_id=1, source_target_pairs={{0,24},{8,32},{16,40},{24,48},{32,56},{40,64},{48,72},{56,80},{64,... | collective-permute-start | bytes 10376 | tf_op jit(solution)/shard_map/ppermute | solution.py:18
  381.5 1.3 collective-permute-start.5
  382.8 0.7 collective-permute-done.5
  383.5 0.6 slice_bitcast_fusion.3
  (152 shorter events, 9.8 us)
Async XLA Ops:
  7.2 7.2 %copy-start.5 = (f32[1,8192]{1,0:T(1,128)S(1)}, f32[1,8192]{1,0:T(1,128)}, u32[]{:S(2)}) copy-start(f32[1,8192]{1,0:T(1,128)} %param.10) | copy-start | bytes 98308
  7.2 94.0 %all-gather.5.cloned.1.call-start = ((), (), s32[]{:S(2)}) async-start(), calls=%async_computation.1 | async-start | bytes 4325376 | tf_op jit(solution)/shard_map/all_gather | solution.py:100
  7.9 199.6 %all-gather.3.cloned.1.call-start = ((), (), s32[]{:S(2)}) async-start(), calls=%async_computation | async-start | bytes 8650752 | tf_op jit(solution)/shard_map/all_gather | solution.py:99
  10.3 4.1 %copy-start = (bf16[2,144,8192]{2,1,0:T(8,128)(2,1)S(1)}, bf16[2,144,8192]{2,1,0:T(8,128)(2,1)}, u32[]{:S(2)}) copy-start(bf16[2,144,8192]{2,1,0:T(8,128)(2,1)} %param.9) | copy-start | bytes 14155780
  226.0 1.9 copy-start.6
  226.6 18.7 %collective-permute-start = (bf16[2,144,768]{2,1,0:T(8,128)(2,1)S(1)}, bf16[2,144,768]{2,1,0:T(8,128)(2,1)S(1)}, u32[]{:S(2)}, u32[]{:S(2)}) collective-permute-start(bf16[2,144,768]{2,1,0:T(8,128)(2,1)S(1)} %get-tuple-element.96), channel_id=1, source_target_pairs={{8,0},{16,8},{24,16},{32,24},{40,32},{48,40},{56,48},{64,56},{72,6... | collective-permute-start | bytes 1327112 | tf_op jit(solution)/shard_map/ppermute | solution.py:18
  227.9 23.5 %collective-permute-start.1 = (bf16[2,144,768]{2,1,0:T(8,128)(2,1)S(1)}, bf16[2,144,768]{2,1,0:T(8,128)(2,1)S(1)}, u32[]{:S(2)}, u32[]{:S(2)}) collective-permute-start(bf16[2,144,768]{2,1,0:T(8,128)(2,1)S(1)} %get-tuple-element.96), channel_id=1, source_target_pairs={{16,0},{24,8},{32,16},{40,24},{48,32},{56,40},{64,48},{72,56},{80,... | collective-permute-start | bytes 1327112 | tf_op jit(solution)/shard_map/ppermute | solution.py:18
  229.2 22.2 %collective-permute-start.2 = (bf16[2,144,768]{2,1,0:T(8,128)(2,1)S(1)}, bf16[2,144,768]{2,1,0:T(8,128)(2,1)S(1)}, u32[]{:S(2)}, u32[]{:S(2)}) collective-permute-start(bf16[2,144,768]{2,1,0:T(8,128)(2,1)S(1)} %get-tuple-element.96), channel_id=1, source_target_pairs={{24,0},{32,8},{40,16},{48,24},{56,32},{64,40},{72,48},{80,56},{88,... | collective-permute-start | bytes 1327112 | tf_op jit(solution)/shard_map/ppermute | solution.py:18
  230.7 45.6 %collective-permute-start.3 = (bf16[2,144,768]{2,1,0:T(8,128)(2,1)S(1)}, bf16[2,144,768]{2,1,0:T(8,128)(2,1)S(1)}, u32[]{:S(2)}, u32[]{:S(2)}) collective-permute-start(bf16[2,144,768]{2,1,0:T(8,128)(2,1)S(1)} %get-tuple-element.96), channel_id=1, source_target_pairs={{32,0},{40,8},{48,16},{56,24},{64,32},{72,40},{80,48},{88,56},{96,... | collective-permute-start | bytes 1327112 | tf_op jit(solution)/shard_map/ppermute | solution.py:18
  276.3 1.4 copy-start.1
  280.4 17.2 %copy-start.7 = (f32[512]{0:T(512)S(1)}, f32[512]{0:T(512)}, u32[]{:S(2)}) copy-start(f32[512]{0:T(512)} %param.13) | copy-start | bytes 6148
  281.3 2.5 copy-start.4
  283.8 3.5 copy-start.2
  287.4 1.6 copy-start.3
  289.8 2.5 copy-start.4
  292.3 3.5 copy-start.2
  296.0 1.6 copy-start.3
  371.2 11.6 %collective-permute-start.4 = (f32[2,144,3]{1,0,2:T(2,128)S(1)}, f32[2,144,3]{1,0,2:T(2,128)S(1)}, u32[]{:S(2)}, u32[]{:S(2)}) collective-permute-start(f32[2,144,3]{1,0,2:T(2,128)S(1)} %get-tuple-element.106), channel_id=1, source_target_pairs={{0,8},{8,16},{16,24},{24,32},{32,40},{40,48},{48,56},{56,64},{64,7... | collective-permute-start | bytes 10376 | tf_op jit(solution)/shard_map/ppermute | solution.py:18
  372.5 10.3 %collective-permute-start.7 = (f32[2,144,3]{1,0,2:T(2,128)S(1)}, f32[2,144,3]{1,0,2:T(2,128)S(1)}, u32[]{:S(2)}, u32[]{:S(2)}) collective-permute-start(f32[2,144,3]{1,0,2:T(2,128)S(1)} %get-tuple-element.107), channel_id=1, source_target_pairs={{0,32},{8,40},{16,48},{24,56},{32,64},{40,72},{48,80},{56,88},{64,... | collective-permute-start | bytes 10376 | tf_op jit(solution)/shard_map/ppermute | solution.py:18
  374.8 7.9 %collective-permute-start.6 = (f32[2,144,3]{1,0,2:T(2,128)S(1)}, f32[2,144,3]{1,0,2:T(2,128)S(1)}, u32[]{:S(2)}, u32[]{:S(2)}) collective-permute-start(f32[2,144,3]{1,0,2:T(2,128)S(1)} %get-tuple-element.108), channel_id=1, source_target_pairs={{0,24},{8,32},{16,40},{24,48},{32,56},{40,64},{48,72},{56,80},{64,... | collective-permute-start | bytes 10376 | tf_op jit(solution)/shard_map/ppermute | solution.py:18
  381.5 2.1 collective-permute-start.5
Sparse Core Ops, SparseCore 0:
  11.2 89.9 all-gather.4
  104.3 103.2 all-gather.2
where the time goes:
time: 396 us; the launch traced here: 391 us
  waiting for transfers between devices  230 us (58%)
  blocking collectives  56 us (14%)
  local copies, waits for them, and re-layouts  33.8 us (9%)
  matrix products  26.6 us (7%)
  starting transfers between devices  17 us (4%)
  between operations  14.7 us (4%)
  other arithmetic  12.8 us (3%)
    all_gather x1, waiting for transfers between devices, on_device(): lax.all_gather(query_weight, 'seq', axis=1, tiled=True)  101 us
    all_gather x1, waiting for transfers between devices, on_device(): lax.all_gather(keyvalue_weight, 'seq', axis=1, tiled=True)  83.3 us
    psum x1, blocking collectives, on_device(): summed = lax.psum(partial_sums, ('sec', 'mp'))  56 us
    ppermute x8, waiting for transfers between devices, shifted(): return lax.ppermute(block, axis, route)  44.6 us
    ppermute x8, starting transfers between devices, shifted(): return lax.ppermute(block, axis, route)  16.9 us
    dot_general x1, local copies, waits for them, and re-layouts, project_piece(): jnp.dot(normed, piece.reshape(piece.shape[0], -1), preferred_element_type...  11.9 us
    dot_general x2, matrix products, project_piece(): jnp.dot(normed, piece.reshape(piece.shape[0], -1), preferred_element_type...  11.5 us
  transfers between devices with their start and end apart: 10, of which 6 were waited for; matrix products, arithmetic and copies ran while one was open for 4% of the time, Pallas kernels for 0%

commit v1 on v0

v1 whole, which is shorter than its diff:
```python
import functools

import jax
import jax.numpy as jnp
from jax import lax
from jax.experimental import pallas as pl
from jax.experimental.pallas import tpu as pltpu
from jax.sharding import PartitionSpec as P

F32 = jnp.float32
BF16 = jnp.bfloat16
MESH = pl.DeviceIdType.MESH
HIGHEST = lax.Precision.HIGHEST

HD = 128
NX, NY, NZ = 4, 8, 8
ROWS = 144
BLOCK = 288
GROUP = 576
WINDOW = 864
WIDTH = 8192
PIECE = 256
NRESP = 64
LAMBDA_GAE = 0.95
LOG_LAMBDA = -0.05129329438755058
LOG_BASE = 13.815510557964274
NORM_EPS = 1e-06
SCALE = float(HD) ** -0.5

REL = (0, 1, -1, 2, -2, 3, -3, 4)
PLACE = {0: 0, 1: 1, -1: 2, 2: 3, -2: 4, 3: 5, -3: 6, 4: 7, -4: 7}


def rel_of(place):
    return ((place + 1) // 2) * (2 * (place % 2) - 1)


def remote(src, dst, send, recv, device):
    copy = pltpu.make_async_remote_copy(
        src_ref=src, dst_ref=dst, send_sem=send, recv_sem=recv, device_id=device, device_id_type=MESH
    )
    copy.start()


def local(src, dst, sem):
    pltpu.make_async_copy(src, dst, sem).start()


def take(ref, sem):
    pltpu.make_async_copy(ref, ref, sem).wait()


def iota(shape, axis):
    return lax.broadcasted_iota(jnp.int32, shape, axis)


def dot(a, b, over, precision=None):
    return lax.dot_general(
        a, b, ((over[0], over[1]), ((), ())), precision=precision, preferred_element_type=F32
    )


def closing_row(lengths):
    upto = (iota((NRESP, NRESP), 0) <= iota((NRESP, NRESP), 1)).astype(F32)
    return dot(lengths, upto, ((1,), (0,)), HIGHEST)


def closing_column(lengths):
    upto = (iota((NRESP, NRESP), 1) <= iota((NRESP, NRESP), 0)).astype(F32)
    return dot(upto, lengths, ((1,), (1,)), HIGHEST)


def places():
    s = lax.axis_index("sec")
    q = lax.axis_index("seq")
    z = lax.axis_index("mp")
    return s, q % NX, q // NX, z


def at(s, x, y, z):
    return (s, y * NX + x, z)


def section_kernel(
    hid, gain, qw, kvw, policy, critic, lengths, out,
    hbuf, raw, normed, wts, scales, own, side, rs_out, rs_in, rl_out, rl_in,
    queries, window, attended,
    sem_loc, send_a, recv_a, send_d, recv_d, send_z, recv_z, send_c, recv_c,
    send_s, recv_s, send_b, recv_b, send_l, recv_l, send_r, recv_r, send_h, recv_h,
):
    s, x, y, z = places()
    micro, half = x // 2, x % 2
    other = 1 - s

    def chip(dx=0, dy=0):
        return at(s, (x + dx + NX) % NX, (y + dy + NY) % NY, z)

    diagonal = at(s, 2 * micro + 1 - half, (y + 2 * half - 1 + NY) % NY, z)
    ring_z = [at(s, x, y, (z + 1) % NZ), at(s, x, y, (z + NZ - 1) % NZ)]
    ring_y = [chip(dy=1), chip(dy=-1)]
    sibling = at(other, x, y, z)

    barrier = pltpu.get_barrier_semaphore()
    partners = [at((s + ds) % 2, (x + dx) % NX, y, z) for ds in range(2) for dx in range(NX)][1:]
    partners = partners + ring_y + ring_z + [diagonal]
    for device in partners:
        pl.semaphore_signal(barrier, inc=1, device_id=device, device_id_type=MESH)
    pl.semaphore_wait(barrier, len(partners))

    def column(place, xx):
        start = ((y + rel_of(place) + NY) % NY) * (NX * PIECE) + xx * PIECE
        return pl.ds(pl.multiple_of(start, PIECE), PIECE)

    facing = (x + 2) % NX
    remote(hid.at[s, :, column(z, facing)], raw.at[0, 2, z], send_d, recv_d, chip(dx=2))
    local(hid.at[s], hbuf, sem_loc.at[0])

    def weights(c, place, piece=None):
        begin, size = place * PIECE, PIECE
        if piece is not None:
            begin, size = begin + piece * (PIECE // 2), PIECE // 2
        return wts.at[c, pl.ds(begin, size)]

    mine = (kvw, qw.at[:, pl.ds(0, PIECE)], qw.at[:, pl.ds(PIECE, PIECE)])

    def ring_send(c, step):
        for d, sign in ((0, 1), (1, -1)):
            piece = d if step == 4 else None
            target = weights(c, PLACE[-sign * step], piece)
            source = mine[c] if step == 1 else weights(c, PLACE[-sign * (step - 1)], piece)
            remote(source, target, send_b.at[c, step - 1, d], recv_b.at[c, step - 1, d], ring_y[d])

    def ring_take(c, step, sems=None):
        sems = recv_b if sems is None else sems
        for d, sign in ((0, 1), (1, -1)):
            piece = d if step == 4 else None
            take(weights(c, PLACE[-sign * step], piece), sems.at[c, step - 1, d])

    ring_send(0, 1)

    for place in range(NY):
        for d, dx in ((0, 1), (1, NX - 1)):
            remote(
                hid.at[s, :, column(place, (x + dx) % NX)],
                raw.at[0, NX - dx, place],
                send_a.at[d],
                recv_a.at[d],
                chip(dx=dx),
            )
        if place == 1:
            ring_send(1, 1)
    for place in range(NY):
        local(hid.at[s, :, column(place, x)], raw.at[0, 0, place], sem_loc.at[1])
        local(hid.at[other, :, column(place, x)], raw.at[1, 0, place], sem_loc.at[2])
    for c in range(3):
        local(mine[c], weights(c, 0), sem_loc.at[3 + c])

    take(hbuf, sem_loc.at[0])

    def squares(i, total):
        for j in range(4):
            start = pl.multiple_of((i * 4 + j) * HD, HD)
            part = hbuf[:, pl.ds(start, HD)].astype(F32)
            total = total + part * part
        return total

    total = lax.fori_loop(0, WIDTH // HD // 4, squares, jnp.zeros((ROWS, HD), F32))
    mean = dot(jnp.ones((8, HD), F32), total, ((1,), (1,)), HIGHEST) * (1.0 / WIDTH)
    scales[0] = lax.rsqrt(mean + NORM_EPS)
    for ds in range(2):
        for dx in range(NX):
            if ds + dx > 0:
                slot = ((2 - ds) % 2) * NX + (NX - dx) % NX
                remote(
                    scales.at[0], scales.at[slot], send_s, recv_s, at((s + ds) % 2, (x + dx) % NX, y, z)
                )

    def z_shard(index, d, step):
        shard = raw.at[0, 2, (index + 2 * NZ) % NZ]
        if step == 4:
            shard = shard.at[:, pl.ds(d * HD, HD)]
        return shard

    def z_send(step):
        for d, sign in ((0, 1), (1, -1)):
            shard = z_shard(z - sign * (step - 1), d, step)
            remote(shard, shard, send_z.at[step - 1, d], recv_z.at[step - 1, d], ring_z[d])

    def z_take(step, sems=None):
        sems = recv_z if sems is None else sems
        for d, sign in ((0, 1), (1, -1)):
            take(z_shard(z - sign * step, d, step), sems.at[step - 1, d])

    take(raw.at[0, 2, z], recv_d)
    z_send(1)
    ring_take(0, 1)
    ring_send(0, 2)
    ring_send(2, 1)

    lens = lengths[...].astype(F32)
    closings = closing_row(lens)
    openings = closings - lens
    opening_line = jnp.where(micro == 0, openings[0:1], openings[1:2])
    row = (y * GROUP + half * BLOCK + iota((BLOCK, 1), 0)).astype(F32)
    opening = jnp.max(jnp.where(opening_line <= row, opening_line, 0.0), axis=1, keepdims=True)
    lane = iota((1, HD), 1)
    inverse = jnp.exp((lane % (HD // 2)).astype(F32) * (-2.0 * LOG_BASE / HD))
    angle = (row - opening) * inverse
    cosine = jnp.cos(angle)
    sine = jnp.sin(angle) * jnp.where(lane < HD // 2, -1.0, 1.0)

    def rotated(v):
        return (v * cosine + pltpu.roll(v, HD // 2, 1) * sine).astype(BF16)

    take(scales.at[pl.ds(1, 7)], recv_s)

    def normalise(ds, dx):
        base = (((s + ds) % 2) * NX + (x + dx) % NX) * ROWS
        rows = pl.ds(pl.multiple_of(base, 16), ROWS)
        spread = (iota((8, PIECE), 0) == 0).astype(F32)
        scale = dot(scales[ds * NX + dx], spread, ((0,), (0,)), HIGHEST)

        def one(place, carry):
            part = raw[ds, dx, place].astype(F32) * scale * gain[0:1, column(place, x)]
            normed[rows, pl.ds(pl.multiple_of(place * PIECE, PIECE), PIECE)] = part.astype(BF16)
            return carry

        lax.fori_loop(0, NY, one, 0)

    def to_sibling(dx):
        remote(raw.at[0, dx], raw.at[1, dx], send_c.at[dx - 1], recv_c.at[dx - 1], sibling)

    z_take(1)
    z_send(2)
    take(raw.at[0, 0], sem_loc.at[1])
    normalise(0, 0)
    ring_take(0, 2)
    ring_send(0, 3)
    z_take(2)
    z_send(3)
    take(raw.at[1, 0], sem_loc.at[2])
    normalise(1, 0)
    ring_take(1, 1)
    ring_send(1, 2)
    z_take(3)
    z_send(4)
    ring_take(0, 3)
    ring_send(0, 4)
    z_take(4)
    to_sibling(2)
    normalise(0, 2)
    ring_take(2, 1)
    ring_send(2, 2)
    take(raw.at[0, 3], recv_a.at[0])
    to_sibling(3)
    take(raw.at[0, 1], recv_a.at[1])
    to_sibling(1)
    ring_take(1, 2)
    ring_send(1, 3)
    normalise(0, 3)
    normalise(0, 1)
    for dx in (2, 3, 1):
        take(raw.at[1, dx], recv_c.at[dx - 1])
        normalise(1, dx)

    def partial(c, xx):
        rows = pl.ds(pl.multiple_of(xx * BLOCK, 32), BLOCK)
        return dot(normed[rows, :], wts[c], ((1,), (0,)))

    def project(c):
        far = partial(c, facing).astype(BF16)
        for d, dx in ((0, 1), (1, NX - 1)):
            rl_out[c, d] = far[:, d * HD : (d + 1) * HD]
            remote(rl_out.at[c, d], rl_in.at[c, d], send_l.at[c, d], recv_l.at[c, d], chip(dx=dx))
        side[c, 0] = partial(c, (x + 1) % NX)
        side[c, 1] = partial(c, (x + NX - 1) % NX)
        own[c] = partial(c, x)

    def pass_on(c):
        for d, dx in ((0, 1), (1, NX - 1)):
            take(rl_in.at[c, d], recv_l.at[c, d])
            both = slice(d * HD, (d + 1) * HD)
            rest = slice((1 - d) * HD, (2 - d) * HD)
            rs_out[c, d, :, both] = (side[c, d, :, both] + rl_in[c, d].astype(F32)).astype(BF16)
            rs_out[c, d, :, rest] = side[c, d, :, rest].astype(BF16)
            remote(rs_out.at[c, d], rs_in.at[c, d], send_r.at[c, d], recv_r.at[c, d], chip(dx=dx))

    def collect(c):
        for d in range(2):
            take(rs_in.at[c, d], recv_r.at[c, d])
        return own[c] + rs_in[c, 0].astype(F32) + rs_in[c, 1].astype(F32)

    for c in range(3):
        take(weights(c, 0), sem_loc.at[3 + c])

    ring_take(0, 4)
    project(0)
    ring_take(2, 2)
    ring_send(2, 3)
    ring_take(1, 3)
    ring_send(1, 4)
    pass_on(0)
    ring_take(1, 4)
    project(1)
    ring_take(2, 3)
    ring_send(2, 4)

    keyvalue = collect(0)
    window[pl.ds(2 * BLOCK, BLOCK), 0:HD] = rotated(keyvalue[:, 0:HD])
    window[pl.ds(2 * BLOCK, BLOCK), HD : 2 * HD] = keyvalue[:, HD : 2 * HD].astype(BF16)
    next_block = at(s, 2 * micro + 1 - half, (y + half) % NY, z)
    for i, device in ((0, chip(dy=1)), (1, next_block)):
        remote(
            window.at[pl.ds(2 * BLOCK, BLOCK)],
            window.at[pl.ds(i * BLOCK, BLOCK)],
            send_h.at[i],
            recv_h.at[i],
            device,
        )
    pass_on(1)
    ring_take(2, 4)
    project(2)

    def store_queries(c):
        pair = collect(c)
        queries[2 * (c - 1)] = rotated(pair[:, 0:HD])
        queries[2 * (c - 1) + 1] = rotated(pair[:, HD : 2 * HD])

    store_queries(1)
    for i in range(2):
        take(window.at[pl.ds(i * BLOCK, BLOCK)], recv_h.at[i])

    key_row = (y * GROUP + half * BLOCK - GROUP + iota((1, WINDOW), 1)).astype(F32)

    def attend(head):
        scores = dot(queries[head], window[:, 0:HD], ((1,), (1,))) * SCALE
        allowed = (key_row >= opening) & (key_row <= row)
        weight = jnp.where(allowed, jnp.exp(scores), 0.0)
        probs = (weight / jnp.sum(weight, axis=1, keepdims=True)).astype(BF16)
        attended[:, head * HD : (head + 1) * HD] = dot(probs, window[:, HD : 2 * HD], ((1,), (0,)))

    attend(0)
    pass_on(2)
    attend(1)
    store_queries(2)
    attend(2)
    attend(3)

    actor = jnp.where(s == 0, 1.0, 0.0)
    kind = iota((8, 4 * HD), 0)
    heads = jnp.where(kind == 0, policy[...] * actor, 0.0)
    heads = jnp.where(kind == 1, critic[0:1] * (1.0 - actor), heads)
    heads = jnp.where(kind == 2, critic[1:2] * (1.0 - actor), heads)
    out[...] = dot(heads, attended[...], ((1,), (1,)), HIGHEST)

    take(raw.at[0, 2, z], send_d)
    for d, dx in ((0, 1), (1, NX - 1)):
        take(raw.at[0, NX - dx], send_a.at[d])
    take(scales.at[pl.ds(1, 7)], send_s)
    for step in range(1, 5):
        z_take(step, send_z)
        for c in range(3):
            ring_take(c, step, send_b)
    for dx in (1, 2, 3):
        take(raw.at[1, dx], send_c.at[dx - 1])
    for c in range(3):
        for d in range(2):
            take(rl_out.at[c, d], send_l.at[c, d])
            take(rs_out.at[c, d], send_r.at[c, d])
    for i in range(2):
        take(window.at[pl.ds(i * BLOCK, BLOCK)], send_h.at[i])


def score_kernel(part, lengths, scores_out, adv_out, ret_out, terms, blocks, send_t, recv_t, send_g, recv_g):
    s, x, y, z = places()

    def chip(dx=0, dy=0):
        return at(s, (x + dx) % NX, (y + dy + NY) % NY, z)

    others = [(ds, dz) for ds in range(2) for dz in range(NZ)][1:]
    stack = [at((s + ds) % 2, x, y, (z + dz) % NZ) for ds, dz in others]
    barrier = pltpu.get_barrier_semaphore()
    partners = stack + [chip(dx, 0) for dx in range(1, NX)]
    partners = partners + [chip(dx, dy) for dx in range(NX) for dy in (-1, 1)]
    for device in partners:
        pl.semaphore_signal(barrier, inc=1, device_id=device, device_id_type=MESH)
    pl.semaphore_wait(barrier, len(partners))

    for (ds, dz), device in zip(others, stack):
        slot = ((2 - ds) % 2) * NZ + (NZ - dz) % NZ - 1
        remote(part, terms.at[slot], send_t, recv_t, device)

    lens = lengths[...].astype(F32)
    closings = closing_column(lens) - (y * GROUP).astype(F32)

    take(terms, recv_t)
    total = part[...]
    for i in range(15):
        total = total + terms[i]
    blocks[0, x] = total
    sends = [(dx, 0) for dx in range(1, NX)] + [(dx, 1) for dx in range(NX)]
    for dx, back in sends:
        remote(blocks.at[0, x], blocks.at[back, x], send_g.at[back, dx], recv_g.at[back, dx], chip(dx, -back))

    now = (x * ROWS + iota((1, ROWS), 1)).astype(F32)
    ends = []
    for m in range(2):
        line = closings[:, m : m + 1]
        ends.append(jnp.min(jnp.where(line > now, line, 1e9), axis=0, keepdims=True))

    for dx, back in sends:
        take(blocks.at[back, (x + NX - dx) % NX], recv_g.at[back, dx])

    for m in range(2):
        kept = jnp.zeros((8, ROWS), F32)
        summed = jnp.zeros((8, ROWS), F32)
        rewarded = jnp.zeros((8, ROWS), F32)
        for back in range(2):
            for h in range(2):
                block = blocks[back, 2 * m + h]
                then = ((2 * back + h) * BLOCK + iota((BLOCK, 1), 0)).astype(F32)
                ahead = then - now
                inside = (ahead >= 0.0) & (then < ends[m])
                power = jnp.exp(jnp.maximum(ahead, 0.0) * LOG_LAMBDA)
                same = (ahead == 0.0).astype(F32)
                later = power * ((1.0 - LAMBDA_GAE) / LAMBDA_GAE)
                value_part = jnp.where(inside, jnp.where(ahead == 0.0, -1.0, later), 0.0)
                reward_part = jnp.where(inside & (then + 1.0 == ends[m]), power, 0.0)
                if back == 0:
                    kept = kept + dot(block, same, ((1,), (0,)), HIGHEST)
                summed = summed + dot(block, value_part, ((1,), (0,)), HIGHEST)
                rewarded = rewarded + dot(block, reward_part, ((1,), (0,)), HIGHEST)
        advantage = summed[1:2] + rewarded[2:3]
        scores_out[m : m + 1, :] = kept[0:1]
        adv_out[m : m + 1, :] = advantage
        ret_out[m : m + 1, :] = advantage + kept[1:2]

    take(terms, send_t)
    for dx, back in sends:
        take(blocks.at[0, x], send_g.at[back, dx])


def on_device(hidden, norm_gain, query_weight, keyvalue_weight, policy_head, critic_heads, lengths):
    vmem = pl.BlockSpec(memory_space=pltpu.VMEM)
    hbm = pl.BlockSpec(memory_space=pl.ANY)
    dma = pltpu.SemaphoreType.DMA
    part = pl.pallas_call(
        section_kernel,
        out_shape=jax.ShapeDtypeStruct((8, BLOCK), F32),
        in_specs=[hbm, vmem, hbm, hbm, vmem, vmem, vmem],
        out_specs=vmem,
        scratch_shapes=[
            pltpu.VMEM((ROWS, WIDTH), BF16),
            pltpu.VMEM((2, NX, NY, ROWS, PIECE), BF16),
            pltpu.VMEM((2 * GROUP, NY * PIECE), BF16),
            pltpu.VMEM((3, NY * PIECE, PIECE), BF16),
            pltpu.VMEM((8, 8, ROWS), F32),
            pltpu.VMEM((3, BLOCK, PIECE), F32),
            pltpu.VMEM((3, 2, BLOCK, PIECE), F32),
            pltpu.VMEM((3, 2, BLOCK, PIECE), BF16),
            pltpu.VMEM((3, 2, BLOCK, PIECE), BF16),
            pltpu.VMEM((3, 2, BLOCK, HD), BF16),
            pltpu.VMEM((3, 2, BLOCK, HD), BF16),
            pltpu.VMEM((4, BLOCK, HD), BF16),
            pltpu.VMEM((WINDOW, PIECE), BF16),
            pltpu.VMEM((BLOCK, 4 * HD), F32),
            dma((6,)), dma((2,)), dma((2,)), dma, dma, dma((4, 2)), dma((4, 2)), dma((3,)), dma((3,)),
            dma, dma, dma((3, 4, 2)), dma((3, 4, 2)), dma((3, 2)), dma((3, 2)), dma((3, 2)), dma((3, 2)),
            dma((2,)), dma((2,)),
        ],
        compiler_params=pltpu.CompilerParams(
            collective_id=0, has_side_effects=True, vmem_limit_bytes=48 * 1024 * 1024
        ),
        name="section",
    )(
        hidden,
        norm_gain,
        query_weight[0],
        keyvalue_weight[0].reshape(PIECE, 2 * HD),
        policy_head.reshape(1, -1),
        critic_heads,
        lengths,
    )
    line = jax.ShapeDtypeStruct((2, ROWS), F32)
    return pl.pallas_call(
        score_kernel,
        out_shape=(line, line, line),
        in_specs=[vmem, vmem],
        out_specs=(vmem, vmem, vmem),
        scratch_shapes=[
            pltpu.VMEM((15, 8, BLOCK), F32),
            pltpu.VMEM((2, NX, 8, BLOCK), F32),
            dma, dma, dma((2, NX)), dma((2, NX)),
        ],
        compiler_params=pltpu.CompilerParams(collective_id=1, has_side_effects=True),
        name="scores",
    )(part, lengths)


def solution(mesh):
    placed = (
        P(None, "seq", None),
        P("sec", None),
        P("sec", "seq", "mp"),
        P("sec", "seq", None, "mp"),
        P("mp"),
        P(None, "mp"),
        P(),
    )
    return jax.shard_map(
        on_device,
        mesh=mesh,
        in_specs=placed,
        out_specs=(P(None, "seq"), P(None, "seq"), P(None, "seq")),
        check_vma=False,
    )
```

time: 396 us -> 109 us (0.28); the launches traced: 391 us -> 109 us
  waiting for transfers between devices: 230 us -> 0 us
  Pallas kernels: 0 us -> 96.9 us
  blocking collectives: 56 us -> 0 us
  matrix products: 26.6 us -> 0 us
  local copies, waits for them, and re-layouts: 33.8 us -> 11.3 us
  starting transfers between devices: 17 us -> 0 us
  between operations: 14.7 us -> 0.67 us
  other arithmetic: 12.8 us -> 0 us
    all_gather x2 -> x0, waiting for transfers between devices: 184 us -> none  [the longest x1 101 us: on_device(): lax.all_gather(query_weight, 'seq', axis=1, tiled=True)]
    pallas_call x0 -> x2, Pallas kernels: none -> 96.9 us  [the longest x1 74.9 us: on_device(): pl.pallas_call(section_kernel, out_shape=jax.ShapeDtypeStruct((8, BLOCK),...]
    psum x1 -> x0, blocking collectives: 56 us -> none  [on_device(): summed = lax.psum(partial_sums, ('sec', 'mp'))]
    ppermute x8 -> x0, waiting for transfers between devices: 44.6 us -> none  [shifted(): return lax.ppermute(block, axis, route)]
    dot_general x7 -> x0, matrix products: 26.6 us -> none  [the longest x2 11.5 us: project_piece(): jnp.dot(normed, piece.reshape(piece.shape[0], -1), preferred_element_type...]
    ppermute x8 -> x0, starting transfers between devices: 16.9 us -> none  [shifted(): return lax.ppermute(block, axis, route)]
    dot_general x1 -> x0, local copies, waits for them, and re-layouts: 11.9 us -> none  [project_piece(): jnp.dot(normed, piece.reshape(piece.shape[0], -1), preferred_element_type...]
    slice x57 -> x0, local copies, waits for them, and re-layouts: 8.78 us -> none  [the longest x51 7.12 us: advantage_terms(): lax.associative_scan(combine_maps, (decay[..., ::-1], delta[..., ::-1]),...]
  transfers between devices with their start and end apart: 10 -> 0, of which waited for: 6 -> 0; matrix products, arithmetic and copies ran while one was open for 4% -> 0% of each run, Pallas kernels for 0% -> 0%
where the time goes in v1:
time: 109 us
  Pallas kernels  96.9 us (89%)
  local copies, waits for them, and re-layouts  11.3 us (10%)
    pallas_call x1, Pallas kernels, on_device(): pl.pallas_call(section_kernel, out_shape=jax.ShapeDtypeStruct((8, BLOCK),...  74.9 us
    pallas_call x1, Pallas kernels, on_device(): pl.pallas_call(score_kernel, out_shape=(line, line, line), in_specs=[vmem...  22 us
    unnamed x18, local copies, waits for them, and re-layouts  11.3 us

profile of v1, /device:TPU:1, one launch (start us, length us, event | category | flops | bytes accessed | tf_op | source)
XLA Modules:
  0.0 108.9 jit_solution(9067368623371265260)
XLA Ops:
  0.6 0.9 copy.12
  1.6 0.0 copy-start
  1.6 2.3 %copy-done = bf16[2,144,8192]{2,1,0:T(8,128)(2,1)S(1)} copy-done((bf16[2,144,8192]{2,1,0:T(8,128)(2,1)S(1)}, bf16[2,144,8192]{2,1,0:T(8,128)(2,1)}, u32[]{:S(2)}) %copy-start) | copy-done | bytes 4718616
  3.9 0.0 copy-start.1
  3.9 0.9 copy-done.1
  4.8 0.0 copy-start.3
  4.8 0.8 copy-done.3
  5.6 0.0 copy-start.4
  5.6 0.7 copy-done.4
  6.3 0.0 copy-start.5
  6.3 0.7 copy-done.5
  7.0 0.0 copy-start.6
  7.0 0.7 copy-done.6
  7.7 74.9 %section.1.part = f32[8,288]{1,0:T(8,128)S(1)} custom-call(bf16[2,144,8192]{2,1,0:T(8,128)(2,1)S(1)} %copy-done, f32[1,8192]{1,0:T(1,128)S(1)} %copy-done.3, bf16[256,512]{1,0:T(8,128)(2,1)S(1)} %bitcast.8, bf16[256,256]{1,0:T(8,128)(2,1)S(1)} %bitcast.7, f32[1,512]{1,0:T(1,128)S(1)} %bitcast.9, f32[2,512]{1,0:T(2,128)S(1)} %copy-done.4, s32[2,64]{1,0:T(2,128)S(1)} %copy-done.5), custom_call_target="tpu_custom_call" | custom-call | tf_op jit(solution)/shard_map/section/pallas_call | solution.py:447
  82.6 0.0 copy-start.2
  82.6 0.6 copy-done.2
  83.2 22.0 %scores.1 = (f32[2,144]{1,0:T(2,128)}, f32[2,144]{1,0:T(2,128)}, f32[2,144]{1,0:T(2,128)}) custom-call(f32[8,288]{1,0:T(8,128)} %copy-done.2, s32[2,64]{1,0:T(2,128)} %lengths.3), custom_call_target="tpu_custom_call" | custom-call | tf_op jit(solution)/shard_map/scores/pallas_call | solution.py:485
  105.2 1.3 %copy.16 = f32[2,144]{1,0:T(2,128)} copy(f32[2,144]{1,0:T(2,128)} %get-tuple-element.6) | data formatting | bytes 2304
  106.4 1.2 %copy.17 = f32[2,144]{1,0:T(2,128)} copy(f32[2,144]{1,0:T(2,128)} %get-tuple-element.7) | data formatting | bytes 2304
  107.7 1.2 %copy.18 = f32[2,144]{1,0:T(2,128)} copy(f32[2,144]{1,0:T(2,128)} %get-tuple-element.8) | data formatting | bytes 2304
Async XLA Ops:
  1.6 2.3 %copy-start = (bf16[2,144,8192]{2,1,0:T(8,128)(2,1)S(1)}, bf16[2,144,8192]{2,1,0:T(8,128)(2,1)}, u32[]{:S(2)}) copy-start(bf16[2,144,8192]{2,1,0:T(8,128)(2,1)} %hid.1) | copy-start | bytes 14155780
  3.9 0.9 copy-start.1
  4.8 0.8 copy-start.3
  5.6 0.7 copy-start.4
  6.3 0.7 copy-start.5
  7.0 0.7 copy-start.6
  82.6 0.6 copy-start.2

commit v2 on v1

v2 whole, which is shorter than its diff:
```python
import functools

import jax
import jax.numpy as jnp
from jax import lax
from jax.experimental import pallas as pl
from jax.experimental.pallas import tpu as pltpu
from jax.sharding import PartitionSpec as P

F32 = jnp.float32
BF16 = jnp.bfloat16
MESH = pl.DeviceIdType.MESH
HIGHEST = lax.Precision.HIGHEST

HD = 128
NX, NY, NZ = 4, 8, 8
ROWS = 144
BLOCK = 288
GROUP = 576
WINDOW = 864
WIDTH = 8192
PIECE = 256
NRESP = 64
LANES = 384
PIECES = 6
LAMBDA_GAE = 0.95
LOG_LAMBDA = -0.05129329438755058
LOG_BASE = 13.815510557964274
NORM_EPS = 1e-06
SCALE = float(HD) ** -0.5

REL = (0, 1, -1, 2, -2, 3, -3, 4)
PLACE = {0: 0, 1: 1, -1: 2, 2: 3, -2: 4, 3: 5, -3: 6, 4: 7, -4: 7}


def rel_of(place):
    return ((place + 1) // 2) * (2 * (place % 2) - 1)


def remote(src, dst, send, recv, device):
    copy = pltpu.make_async_remote_copy(
        src_ref=src, dst_ref=dst, send_sem=send, recv_sem=recv, device_id=device, device_id_type=MESH
    )
    copy.start()


def local(src, dst, sem):
    pltpu.make_async_copy(src, dst, sem).start()


def take(ref, sem):
    pltpu.make_async_copy(ref, ref, sem).wait()


def iota(shape, axis):
    return lax.broadcasted_iota(jnp.int32, shape, axis)


def dot(a, b, over, precision=None):
    return lax.dot_general(
        a, b, ((over[0], over[1]), ((), ())), precision=precision, preferred_element_type=F32
    )


def chain(refs):
    return jnp.concatenate([refs[i : i + 1] for i in range(3)], axis=1)


def closing_row(lengths):
    upto = (iota((NRESP, NRESP), 0) <= iota((NRESP, NRESP), 1)).astype(F32)
    return dot(lengths, upto, ((1,), (0,)), HIGHEST)


def closing_column(lengths):
    upto = (iota((NRESP, NRESP), 1) <= iota((NRESP, NRESP), 0)).astype(F32)
    return dot(upto, lengths, ((1,), (1,)), HIGHEST)


def places():
    s = lax.axis_index("sec")
    q = lax.axis_index("seq")
    z = lax.axis_index("mp")
    return s, q % NX, q // NX, z


def at(s, x, y, z):
    return (s, y * NX + x, z)


def section_kernel(
    hid, gain_hbm, qw, kvw, policy_hbm, critic_hbm, lengths_hbm, out,
    hbuf, raw, normed, wts, scales, gain, policy, critic, lengths,
    own_kv, own_q, out_kv, in_kv, out_q, in_q, queries, window, attended, part, tile, terms, results, blocks, scores,
    sem_loc, send_a, recv_a, send_d, recv_d, send_z, recv_z, send_c, recv_c, send_s, recv_s, send_b, recv_b,
    send_kv, recv_kv, send_q, recv_q, send_h, recv_h, send_t, recv_t, send_g, recv_g, recv_p,
):
    s, x, y, z = places()
    micro, half = x // 2, x % 2
    other = 1 - s

    def chip(dx=0, dy=0, core=None):
        return at(s if core is None else core, (x + dx) % NX, (y + dy + NY) % NY, z)

    def over_z(dz):
        return at(s, x, y, (z + dz + NZ) % NZ)

    sibling = at(other, x, y, z)
    barrier = pltpu.get_barrier_semaphore()
    partners = [chip(dx, 0, (s + ds) % 2) for ds in range(2) for dx in range(NX)][1:]
    partners = partners + [chip(dx, dy, core) for core in range(2) for dx in range(NX) for dy in (-1, 1)]
    partners = partners + [over_z(dz) for dz in range(1, NZ)]
    for device in partners:
        pl.semaphore_signal(barrier, inc=1, device_id=device, device_id_type=MESH)
    pl.semaphore_wait(barrier, len(partners))

    def column(place, xx):
        start = ((y + rel_of(place) + NY) % NY) * (NX * PIECE) + xx * PIECE
        return pl.ds(pl.multiple_of(start, PIECE), PIECE)

    facing = (x + 2) % NX
    quarter = z % 4
    for i in range(2):
        remote(
            hid.at[s, :, column(2 * quarter + i, facing)], raw.at[0, 2, 2 * quarter + i], send_d, recv_d, chip(2)
        )

    def weights(p, place, piece=None):
        begin, size = place * PIECE, PIECE
        if piece is not None:
            begin, size = begin + piece * (PIECE // 2), PIECE // 2
        return wts.at[p // 2, pl.ds(begin, size), pl.ds((p % 2) * HD, HD)]

    def mine(p):
        return kvw.at[:, pl.ds(p * HD, HD)] if p < 2 else qw.at[:, pl.ds((p - 2) * HD, HD)]

    ring_y = [chip(0, 1), chip(0, -1)]

    def ring_send(p, step):
        for d, sign in ((0, 1), (1, -1)):
            piece = d if step == 4 else None
            target = weights(p, PLACE[-sign * step], piece)
            source = mine(p) if step == 1 else weights(p, PLACE[-sign * (step - 1)], piece)
            remote(source, target, send_b.at[p, step - 1, d], recv_b.at[p, step - 1, d], ring_y[d])

    def ring_take(p, step, sems=None):
        sems = recv_b if sems is None else sems
        for d, sign in ((0, 1), (1, -1)):
            piece = d if step == 4 else None
            take(weights(p, PLACE[-sign * step], piece), sems.at[p, step - 1, d])

    def ring(p, step):
        ring_take(p, step)
        ring_send(p, step + 1)

    def to_neighbours(place):
        for d, dx in ((0, 1), (1, NX - 1)):
            remote(
                hid.at[s, :, column(place, (x + dx) % NX)],
                raw.at[0, NX - dx, place],
                send_a.at[d],
                recv_a.at[d],
                chip(dx),
            )

    ring_send(0, 1)
    ring_send(1, 1)
    for place in range(4):
        to_neighbours(place)
    ring_send(2, 1)
    for place in range(4, NY):
        to_neighbours(place)
    local(hid.at[s], hbuf, sem_loc.at[0])
    local(gain_hbm, gain, sem_loc.at[1])
    local(policy_hbm, policy, sem_loc.at[2])
    local(critic_hbm, critic, sem_loc.at[3])
    local(lengths_hbm, lengths, sem_loc.at[4])
    for place in range(NY):
        local(hid.at[s, :, column(place, x)], raw.at[0, 0, place], sem_loc.at[5])
        local(hid.at[other, :, column(place, x)], raw.at[1, 0, place], sem_loc.at[6])
    local(kvw, wts.at[0, pl.ds(0, PIECE)], sem_loc.at[7])
    for i in range(2):
        local(qw.at[:, pl.ds(i * PIECE, PIECE)], wts.at[i + 1, pl.ds(0, PIECE)], sem_loc.at[8 + i])

    def quarters(t, i=None):
        begin = 2 * ((t + 4) % 4)
        return raw.at[0, 2, pl.ds(begin, 2)] if i is None else raw.at[0, 2, begin + i]

    spread = ((1, None), (-1, None), (2, 1), (-2, 0))
    take(quarters(quarter), recv_d)
    for n, (dz, i) in enumerate(spread):
        remote(quarters(quarter, i), quarters(quarter, i), send_z.at[n], recv_z.at[n], over_z(dz))

    take(hbuf, sem_loc.at[0])

    def squares(i, total):
        for j in range(4):
            start = pl.multiple_of((i * 4 + j) * HD, HD)
            block = hbuf[:, pl.ds(start, HD)].astype(F32)
            total = total + block * block
        return total

    total = lax.fori_loop(0, WIDTH // HD // 4, squares, jnp.zeros((ROWS, HD), F32))
    mean = dot(jnp.ones((8, HD), F32), total, ((1,), (1,)), HIGHEST) * (1.0 / WIDTH)
    scales[0] = lax.rsqrt(mean + NORM_EPS)
    for ds in range(2):
        for dx in range(NX):
            if ds + dx > 0:
                slot = ((2 - ds) % 2) * NX + (NX - dx) % NX
                remote(scales.at[0], scales.at[slot], send_s, recv_s, chip(dx, 0, (s + ds) % 2))

    ring(0, 1)
    ring(1, 1)
    ring(2, 1)

    take(lengths, sem_loc.at[4])
    lens = lengths[...].astype(F32)
    openings = closing_row(lens) - lens
    opening_line = jnp.where(micro == 0, openings[0:1], openings[1:2])
    row = (y * GROUP + half * BLOCK + iota((BLOCK, 1), 0)).astype(F32)
    opening = jnp.max(jnp.where(opening_line <= row, opening_line, 0.0), axis=1, keepdims=True)
    lane = iota((1, HD), 1)
    inverse = jnp.exp((lane % (HD // 2)).astype(F32) * (-2.0 * LOG_BASE / HD))
    angle = (row - opening) * inverse
    cosine = jnp.cos(angle)
    sine = jnp.sin(angle) * jnp.where(lane < HD // 2, -1.0, 1.0)

    def rotated(v):
        return (v * cosine + pltpu.roll(v, HD // 2, 1) * sine).astype(BF16)

    take(policy, sem_loc.at[2])
    take(critic, sem_loc.at[3])
    kind = iota((8, 4 * HD), 0)
    first = jnp.where(s == 0, policy[...], critic[0:1])
    second = jnp.where(s == 0, 0.0, critic[1:2])
    heads = jnp.where(kind == 0, first, jnp.where(kind == 1, second, 0.0))
    attended[pl.ds(BLOCK, LANES - BLOCK), :] = jnp.zeros((LANES - BLOCK, HD), F32)

    take(scales.at[pl.ds(1, 7)], recv_s)
    take(gain, sem_loc.at[1])

    def normalise(ds, dx):
        base = (((s + ds) % 2) * NX + (x + dx) % NX) * ROWS
        rows = pl.ds(pl.multiple_of(base, 16), ROWS)
        first_row = (iota((8, PIECE), 0) == 0).astype(F32)
        scale = dot(scales[ds * NX + dx], first_row, ((0,), (0,)), HIGHEST)

        def one(place, carry):
            block = raw[ds, dx, place].astype(F32) * scale * gain[0:1, column(place, x)]
            normed[rows, pl.ds(pl.multiple_of(place * PIECE, PIECE), PIECE)] = block.astype(BF16)
            return carry

        lax.fori_loop(0, NY, one, 0)

    def to_sibling(dx):
        remote(raw.at[0, dx], raw.at[1, dx], send_c.at[dx - 1], recv_c.at[dx - 1], sibling)

    def from_sibling(dx):
        take(raw.at[1, dx], recv_c.at[dx - 1])
        normalise(1, dx)

    take(raw.at[0, 0], sem_loc.at[5])
    normalise(0, 0)
    ring(0, 2)
    take(raw.at[1, 0], sem_loc.at[6])
    normalise(1, 0)
    ring(1, 2)
    ring(2, 2)
    ring(0, 3)
    ring_send(3, 1)
    take(raw.at[0, 3], recv_a.at[0])
    to_sibling(3)
    normalise(0, 3)
    ring(1, 3)
    ring_send(4, 1)
    take(raw.at[0, 1], recv_a.at[1])
    to_sibling(1)
    normalise(0, 1)
    ring(2, 3)
    ring_send(5, 1)
    for n, (dz, i) in enumerate(spread):
        take(quarters(quarter - dz, i), recv_z.at[n])
    to_sibling(2)
    normalise(0, 2)
    from_sibling(3)
    ring(3, 1)
    from_sibling(1)
    ring(4, 1)
    from_sibling(2)
    ring(5, 1)

    def rows_of(dx):
        return pl.ds(pl.multiple_of(((x + dx) % NX) * BLOCK, 32), BLOCK)

    def project_kv(dx):
        product = dot(normed[rows_of(dx), :], wts[0], ((1,), (0,)))
        if dx == 0:
            own_kv[...] = product
        else:
            out_kv[dx - 1] = product.astype(BF16)
            remote(out_kv.at[dx - 1], in_kv.at[dx - 1], send_kv.at[dx - 1], recv_kv.at[dx - 1], chip(dx))

    def project_q(head, dx):
        piece = wts[1 + head // 2, :, (head % 2) * HD : (head % 2 + 1) * HD]
        product = dot(normed[rows_of(dx), :], piece, ((1,), (0,)))
        if dx == 0:
            own_q[head] = product
        else:
            out_q[head, dx - 1] = product.astype(BF16)
            remote(
                out_q.at[head, dx - 1],
                in_q.at[head, dx - 1],
                send_q.at[head, dx - 1],
                recv_q.at[head, dx - 1],
                chip(dx),
            )

    def query(head):
        for dx in range(3):
            take(in_q.at[head, dx], recv_q.at[head, dx])
        summed = own_q[head]
        for dx in range(3):
            summed = summed + in_q[head, dx].astype(F32)
        queries[head] = rotated(summed)

    for i in range(3):
        take(wts.at[i, pl.ds(0, PIECE)], sem_loc.at[7 + i])
    ring_take(0, 4)
    ring_take(1, 4)
    project_kv(2)
    ring(3, 2)
    project_kv(1)
    project_kv(3)
    ring(4, 2)
    project_kv(0)
    ring(5, 2)
    ring_take(2, 4)
    project_q(0, 2)
    project_q(0, 1)
    ring(3, 3)
    project_q(0, 3)
    project_q(0, 0)
    ring(4, 3)

    for dx in range(3):
        take(in_kv.at[dx], recv_kv.at[dx])
    keyvalue = own_kv[...]
    for dx in range(3):
        keyvalue = keyvalue + in_kv[dx].astype(F32)
    window[pl.ds(2 * BLOCK, BLOCK), 0:HD] = rotated(keyvalue[:, 0:HD])
    window[pl.ds(2 * BLOCK, BLOCK), HD : 2 * HD] = keyvalue[:, HD : 2 * HD].astype(BF16)
    next_block = at(s, 2 * micro + 1 - half, (y + half) % NY, z)
    for i, device in ((0, chip(0, 1)), (1, next_block)):
        remote(
            window.at[pl.ds(2 * BLOCK, BLOCK)],
            window.at[pl.ds(i * BLOCK, BLOCK)],
            send_h.at[i],
            recv_h.at[i],
            device,
        )
    ring(5, 3)
    ring_take(3, 4)
    for dx in (2, 1, 3, 0):
        project_q(1, dx)
    query(0)
    ring_take(4, 4)
    for dx in (2, 1, 3, 0):
        project_q(2, dx)
    query(1)
    ring_take(5, 4)
    for dx in (2, 1, 3, 0):
        project_q(3, dx)
    for i in range(2):
        take(window.at[pl.ds(i * BLOCK, BLOCK)], recv_h.at[i])

    key_row = (y * GROUP + half * BLOCK - GROUP + iota((1, WINDOW), 1)).astype(F32)

    def attend(head):
        logits = dot(queries[head], window[:, 0:HD], ((1,), (1,))) * SCALE
        allowed = (key_row >= opening) & (key_row <= row)
        weight = jnp.where(allowed, jnp.exp(logits), 0.0)
        probs = (weight / jnp.sum(weight, axis=1, keepdims=True)).astype(BF16)
        attended[pl.ds(0, BLOCK), :] = dot(probs, window[:, HD : 2 * HD], ((1,), (0,)))
        product = dot(heads[:, head * HD : (head + 1) * HD], attended[...], ((1,), (1,)), HIGHEST)
        if head == 0:
            part[...] = product
        else:
            part[...] += product

    attend(0)
    attend(1)
    query(2)
    attend(2)

    ends = closing_column(lens)

    def end_of(line, base):
        now = (base + iota((1, LANES), 1)).astype(F32)
        return now, jnp.min(jnp.where(line > now, line, 1e9), axis=0, keepdims=True)

    begin = y * GROUP + half * BLOCK
    now, closing = end_of(jnp.where(micro == 0, ends[:, 0:1], ends[:, 1:2]), begin)
    limit = jnp.minimum(closing, (begin + BLOCK).astype(F32))
    given = y * GROUP + (x // 2) * BLOCK
    carries = []
    for m in range(2):
        there, finish = end_of(ends[:, m : m + 1], given)
        edge = (given + BLOCK).astype(F32)
        decay = jnp.exp(jnp.maximum(edge - 1.0 - there, 0.0) * LOG_LAMBDA)
        decay = jnp.where((finish > edge) & (there < edge), decay, 0.0)
        line = ends[:, m : m + 1]
        beyond = jnp.min(jnp.where(line > edge, line, 1e9), axis=0, keepdims=True)
        through = jnp.where(beyond > edge + BLOCK, LAMBDA_GAE ** (BLOCK - 1), 0.0)
        carries.append((decay, through))

    query(3)
    attend(3)

    rows = [part[k : k + 1, i * HD : (i + 1) * HD] for k in range(2) for i in range(3)]
    tile[...] = jnp.concatenate(rows + [jnp.zeros((2, HD), F32)], axis=0)
    for dz in range(1, NZ):
        remote(tile, terms.at[dz - 1], send_t, recv_t, over_z(dz))
    take(terms, recv_t)
    total = tile[...]
    for i in range(NZ - 1):
        total = total + terms[i]

    value, reward = chain(total[0:3]), chain(total[3:6])
    after = pltpu.roll(value, LANES - 1, 1)
    run = jnp.where(closing == now + 1.0, reward, 0.0) + jnp.where(now + 1.0 < limit, after, 0.0) - value
    for j in range(9):
        step = 2**j
        after = pltpu.roll(run, LANES - step, 1)
        run = run + jnp.where(now + step < limit, LAMBDA_GAE**step * after, 0.0)
    scanned = [total[0:3]] + [run[:, i * HD : (i + 1) * HD] for i in range(3)]
    scanned = jnp.concatenate(scanned + [jnp.zeros((2, HD), F32)], axis=0)
    results[...] = jnp.where(s == 0, total, scanned)

    def deliver(target, core, xc, yc, sem, recv, may_stay):
        if may_stay:
            here = (xc == x) & (yc == y)

            @pl.when(here)
            def _():
                local(results, target, recv)

            @pl.when(jnp.logical_not(here))
            def _():
                remote(results, target, sem, recv, at(core, xc, yc, z))

        else:
            remote(results, target, sem, recv, at(core, xc, yc, z))

    def settle(xc, yc, sem, may_stay):
        if may_stay:

            @pl.when(jnp.logical_not((xc == x) & (yc == y)))
            def _():
                take(results, sem)

        else:
            take(results, sem)

    @pl.when(s == 0)
    def _():
        for i in range(4):
            core, xc = i // 2, 2 * half + i % 2
            deliver(scores.at[micro], core, xc, y, send_g.at[i], recv_p.at[micro], core == 0)

    @pl.when(s == 1)
    def _():
        for k in range(3):
            index = 2 * y + half - k + 2 * NY
            for i in range(4):
                core, xc, yc = i // 2, 2 * (index % 2) + i % 2, (index // 2) % NY
                deliver(
                    blocks.at[micro, k], core, xc, yc, send_g.at[4 * k + i], recv_g.at[micro, k], k < 2 and core == 1
                )

    def outgoing(line):
        return jnp.where(half == 0, line[:, 0:ROWS], line[:, ROWS : 2 * ROWS])

    for m in range(2):
        take(scores.at[m], recv_p.at[m])
        for k in range(3):
            take(blocks.at[m, k], recv_g.at[m, k])
        decay, through = carries[m]
        third = blocks[m, 2, 0:1, 0:1] + LAMBDA_GAE * blocks[m, 2, 3:4, 0:1]
        following = blocks[m, 1, 3:4, 0:1] + through * third
        carry = blocks[m, 1, 0:1, 0:1] + LAMBDA_GAE * following
        value = chain(blocks[m, 0, 0:3])
        advantage = chain(blocks[m, 0, 3:6]) + decay * carry
        out[m : m + 1, :] = outgoing(chain(scores[m, 0:3]))
        out[2 + m : 3 + m, :] = outgoing(advantage)
        out[4 + m : 5 + m, :] = outgoing(advantage + value)

    take(quarters(quarter), send_d)
    for d, dx in ((0, 1), (1, NX - 1)):
        take(raw.at[0, NX - dx], send_a.at[d])
    take(scales.at[pl.ds(1, 7)], send_s)
    for n, (dz, i) in enumerate(spread):
        take(quarters(quarter, i), send_z.at[n])
    for p in range(PIECES):
        for step in range(1, 5):
            ring_take(p, step, send_b)
    for dx in range(3):
        take(raw.at[1, dx + 1], send_c.at[dx])
        take(out_kv.at[dx], send_kv.at[dx])
        for head in range(4):
            take(out_q.at[head, dx], send_q.at[head, dx])
    for i in range(2):
        take(window.at[pl.ds(i * BLOCK, BLOCK)], send_h.at[i])
    take(terms, send_t)

    @pl.when(s == 0)
    def _():
        for i in range(4):
            settle(2 * half + i % 2, y, send_g.at[i], i // 2 == 0)

    @pl.when(s == 1)
    def _():
        for k in range(3):
            index = 2 * y + half - k + 2 * NY
            for i in range(4):
                settle(2 * (index % 2) + i % 2, (index // 2) % NY, send_g.at[4 * k + i], k < 2 and i // 2 == 1)


def split_kernel(lines, scores_out, adv_out, ret_out):
    scores_out[...] = lines[0:2]
    adv_out[...] = lines[2:4]
    ret_out[...] = lines[4:6]


def on_device(hidden, norm_gain, query_weight, keyvalue_weight, policy_head, critic_heads, lengths):
    hbm = pl.BlockSpec(memory_space=pl.ANY)
    dma = pltpu.SemaphoreType.DMA
    vmem = pltpu.VMEM
    lines = pl.pallas_call(
        section_kernel,
        out_shape=jax.ShapeDtypeStruct((8, ROWS), F32),
        in_specs=[hbm] * 7,
        out_specs=pl.BlockSpec(memory_space=pltpu.VMEM),
        scratch_shapes=[
            vmem((ROWS, WIDTH), BF16),
            vmem((2, NX, NY, ROWS, PIECE), BF16),
            vmem((2 * GROUP, NY * PIECE), BF16),
            vmem((3, NY * PIECE, PIECE), BF16),
            vmem((8, 8, ROWS), F32),
            vmem((1, WIDTH), F32),
            vmem((1, 4 * HD), F32),
            vmem((2, 4 * HD), F32),
            vmem((2, NRESP), jnp.int32),
            vmem((BLOCK, PIECE), F32),
            vmem((4, BLOCK, HD), F32),
            vmem((3, BLOCK, PIECE), BF16),
            vmem((3, BLOCK, PIECE), BF16),
            vmem((4, 3, BLOCK, HD), BF16),
            vmem((4, 3, BLOCK, HD), BF16),
            vmem((4, BLOCK, HD), BF16),
            vmem((WINDOW, PIECE), BF16),
            vmem((LANES, HD), F32),
            vmem((8, LANES), F32),
            vmem((8, HD), F32),
            vmem((NZ - 1, 8, HD), F32),
            vmem((8, HD), F32),
            vmem((2, 3, 8, HD), F32),
            vmem((2, 8, HD), F32),
            dma((10,)), dma((2,)), dma((2,)), dma, dma, dma((4,)), dma((4,)), dma((3,)), dma((3,)), dma, dma,
            dma((PIECES, 4, 2)), dma((PIECES, 4, 2)), dma((3,)), dma((3,)), dma((4, 3)), dma((4, 3)),
            dma((2,)), dma((2,)), dma, dma, dma((12,)), dma((2, 3)), dma((2,)),
        ],
        compiler_params=pltpu.CompilerParams(
            collective_id=0, has_side_effects=True, vmem_limit_bytes=60 * 1024 * 1024
        ),
        name="section",
    )(
        hidden,
        norm_gain,
        query_weight[0],
        keyvalue_weight[0].reshape(PIECE, 2 * HD),
        policy_head.reshape(1, -1),
        critic_heads,
        lengths,
    )
    line = jax.ShapeDtypeStruct((2, ROWS), F32)
    return pl.pallas_call(split_kernel, out_shape=(line, line, line), name="split")(lines)


def solution(mesh):
    placed = (
        P(None, "seq", None),
        P("sec", None),
        P("sec", "seq", "mp"),
        P("sec", "seq", None, "mp"),
        P("mp"),
        P(None, "mp"),
        P(),
    )
    return jax.shard_map(
        on_device,
        mesh=mesh,
        in_specs=placed,
        out_specs=(P(None, "seq"), P(None, "seq"), P(None, "seq")),
        check_vma=False,
    )
```

time: 109 us -> 90.3 us (0.83)
  local copies, waits for them, and re-layouts: 11.3 us -> 1.56 us
  Pallas kernels: 96.9 us -> 87.9 us
    unnamed x18 -> x1, local copies, waits for them, and re-layouts: 11.3 us -> 1.56 us
    pallas_call x2, Pallas kernels: 96.9 us -> 87.9 us  [the longest x1 86.6 us: on_device(): pl.pallas_call(section_kernel, out_shape=jax.ShapeDtypeStruct((8, ROWS),...]
where the time goes in v2:
time: 90.3 us; the launch traced here: 90.1 us
  Pallas kernels  87.9 us (97%)
  local copies, waits for them, and re-layouts  1.56 us (2%)
    pallas_call x1, Pallas kernels, on_device(): pl.pallas_call(section_kernel, out_shape=jax.ShapeDtypeStruct((8, ROWS),...  86.6 us

profile of v2, /device:TPU:1, one launch (start us, length us, event | category | flops | bytes accessed | tf_op | source)
XLA Modules:
  0.0 90.1 jit_solution(30580249391345469)
XLA Ops:
  0.6 1.6 %copy.12 = bf16[32,8,2,128]{3,1,2,0:T(8,128)(2,1)} copy(bf16[32,8,2,128]{3,2,1,0:T(2,128)(2,1)} %bitcast.9) | data formatting | bytes 262144
  2.2 86.6 %section.1.lines = f32[8,144]{1,0:T(8,128)} custom-call(bf16[2,144,8192]{2,1,0:T(8,128)(2,1)} %hid.1, f32[1,8192]{1,0:T(1,128)} %gain_hbm.1, bf16[256,512]{1,0:T(8,128)(2,1)} %bitcast.8, bf16[256,256]{1,0:T(8,128)(2,1)} %bitcast.7, f32[1,512]{1,0:T(1,128)} %bitcast.10, f32[2,512]{1,0:T(2,128)} %critic_hbm.1, s32[2,64]{1,0:T(2,128)} %lengths_hbm.1), custom_call_target="tpu_custom_call" | custom-call | tf_op jit(solution)/shard_map/section/pallas_call | solution.py:537
  88.8 1.3 %split.1 = (f32[2,144]{1,0:T(2,128)}, f32[2,144]{1,0:T(2,128)}, f32[2,144]{1,0:T(2,128)}) custom-call(f32[8,144]{1,0:T(8,128)} %section.1.lines), custom_call_target="tpu_custom_call" | custom-call | tf_op jit(solution)/shard_map/split/pallas_call | solution.py:585

commit v3 on v2

--- a/solution.py
+++ b/solution.py
@@ -89,7 +89,7 @@
 
 def section_kernel(
     hid, gain_hbm, qw, kvw, policy_hbm, critic_hbm, lengths_hbm, out,
-    hbuf, raw, normed, wts, scales, gain, policy, critic, lengths,
+    hbuf, raw, normed, pairs, wts, scales, gain, policy, critic, lengths,
     own_kv, own_q, out_kv, in_kv, out_q, in_q, queries, window, attended, part, tile, terms, results, blocks, scores,
     sem_loc, send_a, recv_a, send_d, recv_d, send_z, recv_z, send_c, recv_c, send_s, recv_s, send_b, recv_b,
     send_kv, recv_kv, send_q, recv_q, send_h, recv_h, send_t, recv_t, send_g, recv_g, recv_p,
@@ -111,18 +111,41 @@
     partners = partners + [over_z(dz) for dz in range(1, NZ)]
     for device in partners:
         pl.semaphore_signal(barrier, inc=1, device_id=device, device_id_type=MESH)
-    pl.semaphore_wait(barrier, len(partners))
-
     def column(place, xx):
         start = ((y + rel_of(place) + NY) % NY) * (NX * PIECE) + xx * PIECE
         return pl.ds(pl.multiple_of(start, PIECE), PIECE)
 
-    facing = (x + 2) % NX
-    quarter = z % 4
+    local(hid.at[s], hbuf, sem_loc.at[0])
+    local(kvw, pairs, sem_loc.at[7])
+    local(gain_hbm, gain, sem_loc.at[1])
+    local(policy_hbm, policy, sem_loc.at[2])
+    local(critic_hbm, critic, sem_loc.at[3])
+    local(lengths_hbm, lengths, sem_loc.at[4])
+    for place in range(NY):
+        local(hid.at[s, :, column(place, x)], raw.at[0, 0, place], sem_loc.at[5])
+        local(hid.at[other, :, column(place, x)], raw.at[1, 0, place], sem_loc.at[6])
     for i in range(2):
-        remote(
-            hid.at[s, :, column(2 * quarter + i, facing)], raw.at[0, 2, 2 * quarter + i], send_d, recv_d, chip(2)
-        )
+        local(qw.at[:, pl.ds(i * PIECE, PIECE)], wts.at[i + 1, pl.ds(0, PIECE)], sem_loc.at[8 + i])
+
+    take(hbuf, sem_loc.at[0])
+
+    def squares(i, total):
+        for j in range(4):
+            start = pl.multiple_of((i * 4 + j) * HD, HD)
+            block = hbuf[:, pl.ds(start, HD)].astype(F32)
+            total = total + block * block
+        return total
+
+    total = lax.fori_loop(0, WIDTH // HD // 4, squares, jnp.zeros((ROWS, HD), F32))
+    mean = dot(jnp.ones((8, HD), F32), total, ((1,), (1,)), HIGHEST) * (1.0 / WIDTH)
+    scales[0] = lax.rsqrt(mean + NORM_EPS)
+    take(pairs, sem_loc.at[7])
+    for i in range(2):
+        chosen = iota((PIECE, 2 * PIECE), 1) == 2 * iota((PIECE, 2 * PIECE), 0) + i
+        sorted_rows = dot(chosen.astype(F32).astype(BF16), pairs[...], ((1,), (0,)))
+        wts[0, 0:PIECE, i * HD : (i + 1) * HD] = sorted_rows.astype(BF16)
+
+    pl.semaphore_wait(barrier, len(partners))
 
     def weights(p, place, piece=None):
         begin, size = place * PIECE, PIECE
@@ -131,26 +154,27 @@
         return wts.at[p // 2, pl.ds(begin, size), pl.ds((p % 2) * HD, HD)]
 
     def mine(p):
-        return kvw.at[:, pl.ds(p * HD, HD)] if p < 2 else qw.at[:, pl.ds((p - 2) * HD, HD)]
+        return weights(p, 0) if p < 2 else qw.at[:, pl.ds((p - 2) * HD, HD)]
 
     ring_y = [chip(0, 1), chip(0, -1)]
 
-    def ring_send(p, step):
-        for d, sign in ((0, 1), (1, -1)):
-            piece = d if step == 4 else None
+    def ring_send(p, step, ways=(0, 1)):
+        for d in ways:
+            sign, piece = 1 - 2 * d, d if step == 4 else None
             target = weights(p, PLACE[-sign * step], piece)
             source = mine(p) if step == 1 else weights(p, PLACE[-sign * (step - 1)], piece)
             remote(source, target, send_b.at[p, step - 1, d], recv_b.at[p, step - 1, d], ring_y[d])
 
-    def ring_take(p, step, sems=None):
+    def ring_take(p, step, sems=None, ways=(0, 1)):
         sems = recv_b if sems is None else sems
-        for d, sign in ((0, 1), (1, -1)):
-            piece = d if step == 4 else None
+        for d in ways:
+            sign, piece = 1 - 2 * d, d if step == 4 else None
             take(weights(p, PLACE[-sign * step], piece), sems.at[p, step - 1, d])
 
     def ring(p, step):
-        ring_take(p, step)
-        ring_send(p, step + 1)
+        for d in range(2):
+            ring_take(p, step, None, (d,))
+            ring_send(p, step + 1, (d,))
 
     def to_neighbours(place):
         for d, dx in ((0, 1), (1, NX - 1)):
@@ -162,54 +186,32 @@
                 chip(dx),
             )
 
-    ring_send(0, 1)
-    ring_send(1, 1)
-    for place in range(4):
-        to_neighbours(place)
-    ring_send(2, 1)
-    for place in range(4, NY):
-        to_neighbours(place)
-    local(hid.at[s], hbuf, sem_loc.at[0])
-    local(gain_hbm, gain, sem_loc.at[1])
-    local(policy_hbm, policy, sem_loc.at[2])
-    local(critic_hbm, critic, sem_loc.at[3])
-    local(lengths_hbm, lengths, sem_loc.at[4])
-    for place in range(NY):
-        local(hid.at[s, :, column(place, x)], raw.at[0, 0, place], sem_loc.at[5])
-        local(hid.at[other, :, column(place, x)], raw.at[1, 0, place], sem_loc.at[6])
-    local(kvw, wts.at[0, pl.ds(0, PIECE)], sem_loc.at[7])
+    for p in range(3):
+        ring_send(p, 1)
+    facing = (x + 2) % NX
+    quarter = z % 4
     for i in range(2):
-        local(qw.at[:, pl.ds(i * PIECE, PIECE)], wts.at[i + 1, pl.ds(0, PIECE)], sem_loc.at[8 + i])
-
-    def quarters(t, i=None):
-        begin = 2 * ((t + 4) % 4)
-        return raw.at[0, 2, pl.ds(begin, 2)] if i is None else raw.at[0, 2, begin + i]
-
-    spread = ((1, None), (-1, None), (2, 1), (-2, 0))
-    take(quarters(quarter), recv_d)
-    for n, (dz, i) in enumerate(spread):
-        remote(quarters(quarter, i), quarters(quarter, i), send_z.at[n], recv_z.at[n], over_z(dz))
-
-    take(hbuf, sem_loc.at[0])
-
-    def squares(i, total):
-        for j in range(4):
-            start = pl.multiple_of((i * 4 + j) * HD, HD)
-            block = hbuf[:, pl.ds(start, HD)].astype(F32)
-            total = total + block * block
-        return total
-
-    total = lax.fori_loop(0, WIDTH // HD // 4, squares, jnp.zeros((ROWS, HD), F32))
-    mean = dot(jnp.ones((8, HD), F32), total, ((1,), (1,)), HIGHEST) * (1.0 / WIDTH)
-    scales[0] = lax.rsqrt(mean + NORM_EPS)
+        remote(
+            hid.at[s, :, column(2 * quarter + i, facing)], raw.at[0, 2, 2 * quarter + i], send_d, recv_d, chip(2)
+        )
     for ds in range(2):
         for dx in range(NX):
             if ds + dx > 0:
                 slot = ((2 - ds) % 2) * NX + (NX - dx) % NX
                 remote(scales.at[0], scales.at[slot], send_s, recv_s, chip(dx, 0, (s + ds) % 2))
+    def quarters(t, i=None):
+        begin = 2 * ((t + 4) % 4)
+        return raw.at[0, 2, pl.ds(begin, 2)] if i is None else raw.at[0, 2, begin + i]
+
+    spread = ((1, None), (-1, None), (2, 1), (-2, 0))
+    for place in range(NY):
+        to_neighbours(place)
 
     ring(0, 1)
     ring(1, 1)
+    take(quarters(quarter), recv_d)
+    for n, (dz, i) in enumerate(spread):
+        remote(quarters(quarter, i), quarters(quarter, i), send_z.at[n], recv_z.at[n], over_z(dz))
     ring(2, 1)
 
     take(lengths, sem_loc.at[4])
@@ -227,6 +229,27 @@
     def rotated(v):
         return (v * cosine + pltpu.roll(v, HD // 2, 1) * sine).astype(BF16)
 
+    ends = closing_column(lens)
+
+    def end_of(line, base):
+        now = (base + iota((1, LANES), 1)).astype(F32)
+        return now, jnp.min(jnp.where(line > now, line, 1e9), axis=0, keepdims=True)
+
+    begin = y * GROUP + half * BLOCK
+    now, closing = end_of(jnp.where(micro == 0, ends[:, 0:1], ends[:, 1:2]), begin)
+    limit = jnp.minimum(closing, (begin + BLOCK).astype(F32))
+    given = y * GROUP + (x // 2) * BLOCK
+    carries = []
+    for m in range(2):
+        there, finish = end_of(ends[:, m : m + 1], given)
+        edge = (given + BLOCK).astype(F32)
+        decay = jnp.exp(jnp.maximum(edge - 1.0 - there, 0.0) * LOG_LAMBDA)
+        decay = jnp.where((finish > edge) & (there < edge), decay, 0.0)
+        line = ends[:, m : m + 1]
+        beyond = jnp.min(jnp.where(line > edge, line, 1e9), axis=0, keepdims=True)
+        through = jnp.where(beyond > edge + BLOCK, LAMBDA_GAE ** (BLOCK - 1), 0.0)
+        carries.append((decay, through))
+
     take(policy, sem_loc.at[2])
     take(critic, sem_loc.at[3])
     kind = iota((8, 4 * HD), 0)
@@ -257,36 +280,6 @@
     def from_sibling(dx):
         take(raw.at[1, dx], recv_c.at[dx - 1])
         normalise(1, dx)
-
-    take(raw.at[0, 0], sem_loc.at[5])
-    normalise(0, 0)
-    ring(0, 2)
-    take(raw.at[1, 0], sem_loc.at[6])
-    normalise(1, 0)
-    ring(1, 2)
-    ring(2, 2)
-    ring(0, 3)
-    ring_send(3, 1)
-    take(raw.at[0, 3], recv_a.at[0])
-    to_sibling(3)
-    normalise(0, 3)
-    ring(1, 3)
-    ring_send(4, 1)
-    take(raw.at[0, 1], recv_a.at[1])
-    to_sibling(1)
-    normalise(0, 1)
-    ring(2, 3)
-    ring_send(5, 1)
-    for n, (dz, i) in enumerate(spread):
-        take(quarters(quarter - dz, i), recv_z.at[n])
-    to_sibling(2)
-    normalise(0, 2)
-    from_sibling(3)
-    ring(3, 1)
-    from_sibling(1)
-    ring(4, 1)
-    from_sibling(2)
-    ring(5, 1)
 
     def rows_of(dx):
         return pl.ds(pl.multiple_of(((x + dx) % NX) * BLOCK, 32), BLOCK)
@@ -322,53 +315,82 @@
             summed = summed + in_q[head, dx].astype(F32)
         queries[head] = rotated(summed)
 
-    for i in range(3):
+    def project(head, order=(2, 1, 3, 0)):
+        for dx in order:
+            if head is None:
+                project_kv(dx)
+            else:
+                project_q(head, dx)
+
+    def key_value():
+        for dx in range(3):
+            take(in_kv.at[dx], recv_kv.at[dx])
+        keyvalue = own_kv[...]
+        for dx in range(3):
+            keyvalue = keyvalue + in_kv[dx].astype(F32)
+        window[pl.ds(2 * BLOCK, BLOCK), 0:HD] = rotated(keyvalue[:, 0:HD])
+        window[pl.ds(2 * BLOCK, BLOCK), HD : 2 * HD] = keyvalue[:, HD : 2 * HD].astype(BF16)
+        next_block = at(s, 2 * micro + 1 - half, (y + half) % NY, z)
+        for i, device in ((0, chip(0, 1)), (1, next_block)):
+            remote(
+                window.at[pl.ds(2 * BLOCK, BLOCK)],
+                window.at[pl.ds(i * BLOCK, BLOCK)],
+                send_h.at[i],
+                recv_h.at[i],
+                device,
+            )
+
+    take(raw.at[0, 0], sem_loc.at[5])
+    take(raw.at[1, 0], sem_loc.at[6])
+    for i in range(1, 3):
         take(wts.at[i, pl.ds(0, PIECE)], sem_loc.at[7 + i])
+    ring(0, 2)
+    normalise(0, 0)
+    ring(1, 2)
+    normalise(1, 0)
+    ring(2, 2)
+    ring(0, 3)
+    ring_send(3, 1)
+    ring(1, 3)
+    ring_send(4, 1)
+    ring(2, 3)
+    for n, (dz, i) in enumerate(spread):
+        take(quarters(quarter - dz, i), recv_z.at[n])
+    to_sibling(2)
+    normalise(0, 2)
+    ring(3, 1)
+    ring_send(5, 1)
+    from_sibling(2)
+    for d, dx in ((0, 3), (1, 1)):
+        take(raw.at[0, dx], recv_a.at[d])
+        to_sibling(dx)
+    ring(4, 1)
+    normalise(0, 3)
+    normalise(0, 1)
+    from_sibling(3)
+    from_sibling(1)
     ring_take(0, 4)
     ring_take(1, 4)
-    project_kv(2)
     ring(3, 2)
-    project_kv(1)
-    project_kv(3)
+    project(None, (2, 1))
+    ring(5, 1)
+    project(None, (3, 0))
     ring(4, 2)
-    project_kv(0)
+    ring_take(2, 4)
+    project(0)
+    ring(3, 3)
     ring(5, 2)
-    ring_take(2, 4)
-    project_q(0, 2)
-    project_q(0, 1)
-    ring(3, 3)
-    project_q(0, 3)
-    project_q(0, 0)
     ring(4, 3)
-
-    for dx in range(3):
-        take(in_kv.at[dx], recv_kv.at[dx])
-    keyvalue = own_kv[...]
-    for dx in range(3):
-        keyvalue = keyvalue + in_kv[dx].astype(F32)
-    window[pl.ds(2 * BLOCK, BLOCK), 0:HD] = rotated(keyvalue[:, 0:HD])
-    window[pl.ds(2 * BLOCK, BLOCK), HD : 2 * HD] = keyvalue[:, HD : 2 * HD].astype(BF16)
-    next_block = at(s, 2 * micro + 1 - half, (y + half) % NY, z)
-    for i, device in ((0, chip(0, 1)), (1, next_block)):
-        remote(
-            window.at[pl.ds(2 * BLOCK, BLOCK)],
-            window.at[pl.ds(i * BLOCK, BLOCK)],
-            send_h.at[i],
-            recv_h.at[i],
-            device,
-        )
+    ring_take(3, 4)
+    project(1)
+    key_value()
     ring(5, 3)
-    ring_take(3, 4)
-    for dx in (2, 1, 3, 0):
-        project_q(1, dx)
+    ring_take(4, 4)
+    project(2)
     query(0)
-    ring_take(4, 4)
-    for dx in (2, 1, 3, 0):
-        project_q(2, dx)
+    ring_take(5, 4)
+    project(3)
     query(1)
-    ring_take(5, 4)
-    for dx in (2, 1, 3, 0):
-        project_q(3, dx)
     for i in range(2):
         take(window.at[pl.ds(i * BLOCK, BLOCK)], recv_h.at[i])
 
@@ -390,27 +412,6 @@
     attend(1)
     query(2)
     attend(2)
-
-    ends = closing_column(lens)
-
-    def end_of(line, base):
-        now = (base + iota((1, LANES), 1)).astype(F32)
-        return now, jnp.min(jnp.where(line > now, line, 1e9), axis=0, keepdims=True)
-
-    begin = y * GROUP + half * BLOCK
-    now, closing = end_of(jnp.where(micro == 0, ends[:, 0:1], ends[:, 1:2]), begin)
-    limit = jnp.minimum(closing, (begin + BLOCK).astype(F32))
-    given = y * GROUP + (x // 2) * BLOCK
-    carries = []
-    for m in range(2):
-        there, finish = end_of(ends[:, m : m + 1], given)
-        edge = (given + BLOCK).astype(F32)
-        decay = jnp.exp(jnp.maximum(edge - 1.0 - there, 0.0) * LOG_LAMBDA)
-        decay = jnp.where((finish > edge) & (there < edge), decay, 0.0)
-        line = ends[:, m : m + 1]
-        beyond = jnp.min(jnp.where(line > edge, line, 1e9), axis=0, keepdims=True)
-        through = jnp.where(beyond > edge + BLOCK, LAMBDA_GAE ** (BLOCK - 1), 0.0)
-        carries.append((decay, through))
 
     query(3)
     attend(3)
@@ -543,6 +544,7 @@
             vmem((ROWS, WIDTH), BF16),
             vmem((2, NX, NY, ROWS, PIECE), BF16),
             vmem((2 * GROUP, NY * PIECE), BF16),
+            vmem((2 * PIECE, HD), BF16),
             vmem((3, NY * PIECE, PIECE), BF16),
             vmem((8, 8, ROWS), F32),
             vmem((1, WIDTH), F32),
@@ -576,7 +578,7 @@
         hidden,
         norm_gain,
         query_weight[0],
-        keyvalue_weight[0].reshape(PIECE, 2 * HD),
+        keyvalue_weight.reshape(2 * PIECE, HD),
         policy_head.reshape(1, -1),
         critic_heads,
         lengths,

time: 90.3 us -> 79.2 us (0.88)
  Pallas kernels: 87.9 us -> 78.4 us
  local copies, waits for them, and re-layouts: 1.56 us -> 0 us
    pallas_call x1, Pallas kernels: 86.6 us -> 77.1 us  [on_device(): pl.pallas_call(section_kernel, out_shape=jax.ShapeDtypeStruct((8, ROWS),...]
    unnamed x1 -> x0, local copies, waits for them, and re-layouts: 1.56 us -> none
where the time goes in v3:
time: 79.2 us; the launch traced here: 79 us
  Pallas kernels  78.4 us (99%)
    pallas_call x1, Pallas kernels, on_device(): pl.pallas_call(section_kernel, out_shape=jax.ShapeDtypeStruct((8, ROWS),...  77.1 us

profile of v3, /device:TPU:1, one launch (start us, length us, event | category | flops | bytes accessed | tf_op | source)
XLA Modules:
  0.0 79.0 jit_solution(15562775202209910461)
XLA Ops:
  0.6 77.1 %section.1.lines = f32[8,144]{1,0:T(8,128)} custom-call(bf16[2,144,8192]{2,1,0:T(8,128)(2,1)} %hid.1, f32[1,8192]{1,0:T(1,128)} %gain_hbm.1, bf16[256,512]{1,0:T(8,128)(2,1)} %bitcast.3, bf16[512,128]{1,0:T(8,128)(2,1)} %bitcast.4, f32[1,512]{1,0:T(1,128)} %bitcast.5, f32[2,512]{1,0:T(2,128)} %critic_hbm.1, s32[2,64]{1,0:T(2,128)} %lengths_hbm.1), custom_call_target="tpu_custom_call" | custom-call | tf_op jit(solution)/shard_map/section/pallas_call | solution.py:538
  77.7 1.3 %split.1 = (f32[2,144]{1,0:T(2,128)}, f32[2,144]{1,0:T(2,128)}, f32[2,144]{1,0:T(2,128)}) custom-call(f32[8,144]{1,0:T(8,128)} %section.1.lines), custom_call_target="tpu_custom_call" | custom-call | tf_op jit(solution)/shard_map/split/pallas_call | solution.py:587

commit v4 on v3

--- a/solution.py
+++ b/solution.py
@@ -381,9 +381,9 @@
     ring(3, 3)
     ring(5, 2)
     ring(4, 3)
+    key_value()
     ring_take(3, 4)
     project(1)
-    key_value()
     ring(5, 3)
     ring_take(4, 4)
     project(2)

time: 79.2 us -> 77.6 us (0.980)
  Pallas kernels: 78.4 us -> 76.8 us
    pallas_call x1, Pallas kernels: 77.1 us -> 75.5 us  [on_device(): pl.pallas_call(section_kernel, out_shape=jax.ShapeDtypeStruct((8, ROWS),...]
where the time goes in v4:
time: 77.6 us; the launch traced here: 77.5 us
  Pallas kernels  76.8 us (99%)
    pallas_call x1, Pallas kernels, on_device(): pl.pallas_call(section_kernel, out_shape=jax.ShapeDtypeStruct((8, ROWS),...  75.5 us

profile of v4, /device:TPU:1, one launch (start us, length us, event | category | flops | bytes accessed | tf_op | source)
XLA Modules:
  0.0 77.5 jit_solution(10853620446226337751)
XLA Ops:
  0.6 75.5 %section.1.lines = f32[8,144]{1,0:T(8,128)} custom-call(bf16[2,144,8192]{2,1,0:T(8,128)(2,1)} %hid.1, f32[1,8192]{1,0:T(1,128)} %gain_hbm.1, bf16[256,512]{1,0:T(8,128)(2,1)} %bitcast.3, bf16[512,128]{1,0:T(8,128)(2,1)} %bitcast.4, f32[1,512]{1,0:T(1,128)} %bitcast.5, f32[2,512]{1,0:T(2,128)} %critic_hbm.1, s32[2,64]{1,0:T(2,128)} %lengths_hbm.1), custom_call_target="tpu_custom_call" | custom-call | tf_op jit(solution)/shard_map/section/pallas_call | solution.py:538
  76.2 1.3 %split.1 = (f32[2,144]{1,0:T(2,128)}, f32[2,144]{1,0:T(2,128)}, f32[2,144]{1,0:T(2,128)}) custom-call(f32[8,144]{1,0:T(8,128)} %section.1.lines), custom_call_target="tpu_custom_call" | custom-call | tf_op jit(solution)/shard_map/split/pallas_call | solution.py:587

commit v5 on v4

--- a/solution.py
+++ b/solution.py
@@ -420,79 +420,6 @@
     tile[...] = jnp.concatenate(rows + [jnp.zeros((2, HD), F32)], axis=0)
     for dz in range(1, NZ):
         remote(tile, terms.at[dz - 1], send_t, recv_t, over_z(dz))
-    take(terms, recv_t)
-    total = tile[...]
-    for i in range(NZ - 1):
-        total = total + terms[i]
-
-    value, reward = chain(total[0:3]), chain(total[3:6])
-    after = pltpu.roll(value, LANES - 1, 1)
-    run = jnp.where(closing == now + 1.0, reward, 0.0) + jnp.where(now + 1.0 < limit, after, 0.0) - value
-    for j in range(9):
-        step = 2**j
-        after = pltpu.roll(run, LANES - step, 1)
-        run = run + jnp.where(now + step < limit, LAMBDA_GAE**step * after, 0.0)
-    scanned = [total[0:3]] + [run[:, i * HD : (i + 1) * HD] for i in range(3)]
-    scanned = jnp.concatenate(scanned + [jnp.zeros((2, HD), F32)], axis=0)
-    results[...] = jnp.where(s == 0, total, scanned)
-
-    def deliver(target, core, xc, yc, sem, recv, may_stay):
-        if may_stay:
-            here = (xc == x) & (yc == y)
-
-            @pl.when(here)
-            def _():
-                local(results, target, recv)
-
-            @pl.when(jnp.logical_not(here))
-            def _():
-                remote(results, target, sem, recv, at(core, xc, yc, z))
-
-        else:
-            remote(results, target, sem, recv, at(core, xc, yc, z))
-
-    def settle(xc, yc, sem, may_stay):
-        if may_stay:
-
-            @pl.when(jnp.logical_not((xc == x) & (yc == y)))
-            def _():
-                take(results, sem)
-
-        else:
-            take(results, sem)
-
-    @pl.when(s == 0)
-    def _():
-        for i in range(4):
-            core, xc = i // 2, 2 * half + i % 2
-            deliver(scores.at[micro], core, xc, y, send_g.at[i], recv_p.at[micro], core == 0)
-
-    @pl.when(s == 1)
-    def _():
-        for k in range(3):
-            index = 2 * y + half - k + 2 * NY
-            for i in range(4):
-                core, xc, yc = i // 2, 2 * (index % 2) + i % 2, (index // 2) % NY
-                deliver(
-                    blocks.at[micro, k], core, xc, yc, send_g.at[4 * k + i], recv_g.at[micro, k], k < 2 and core == 1
-                )
-
-    def outgoing(line):
-        return jnp.where(half == 0, line[:, 0:ROWS], line[:, ROWS : 2 * ROWS])
-
-    for m in range(2):
-        take(scores.at[m], recv_p.at[m])
-        for k in range(3):
-            take(blocks.at[m, k], recv_g.at[m, k])
-        decay, through = carries[m]
-        third = blocks[m, 2, 0:1, 0:1] + LAMBDA_GAE * blocks[m, 2, 3:4, 0:1]
-        following = blocks[m, 1, 3:4, 0:1] + through * third
-        carry = blocks[m, 1, 0:1, 0:1] + LAMBDA_GAE * following
-        value = chain(blocks[m, 0, 0:3])
-        advantage = chain(blocks[m, 0, 3:6]) + decay * carry
-        out[m : m + 1, :] = outgoing(chain(scores[m, 0:3]))
-        out[2 + m : 3 + m, :] = outgoing(advantage)
-        out[4 + m : 5 + m, :] = outgoing(advantage + value)
 
     take(quarters(quarter), send_d)
     for d, dx in ((0, 1), (1, NX - 1)):
@@ -510,6 +437,81 @@
             take(out_q.at[head, dx], send_q.at[head, dx])
     for i in range(2):
         take(window.at[pl.ds(i * BLOCK, BLOCK)], send_h.at[i])
+
+    take(terms, recv_t)
+    total = tile[...]
+    for i in range(NZ - 1):
+        total = total + terms[i]
+
+    value, reward = chain(total[0:3]), chain(total[3:6])
+    after = pltpu.roll(value, LANES - 1, 1)
+    run = jnp.where(closing == now + 1.0, reward, 0.0) + jnp.where(now + 1.0 < limit, after, 0.0) - value
+    for j in range(9):
+        step = 2**j
+        after = pltpu.roll(run, LANES - step, 1)
+        run = run + jnp.where(now + step < limit, LAMBDA_GAE**step * after, 0.0)
+    scanned = [total[0:3]] + [run[:, i * HD : (i + 1) * HD] for i in range(3)]
+    scanned = jnp.concatenate(scanned + [jnp.zeros((2, HD), F32)], axis=0)
+    results[...] = jnp.where(s == 0, total, scanned)
+
+    def deliver(target, core, xc, yc, sem, recv, may_stay):
+        if may_stay:
+            here = (xc == x) & (yc == y)
+
+            @pl.when(here)
+            def _():
+                local(results, target, recv)
+
+            @pl.when(jnp.logical_not(here))
+            def _():
+                remote(results, target, sem, recv, at(core, xc, yc, z))
+
+        else:
+            remote(results, target, sem, recv, at(core, xc, yc, z))
+
+    def settle(xc, yc, sem, may_stay):
+        if may_stay:
+
+            @pl.when(jnp.logical_not((xc == x) & (yc == y)))
+            def _():
+                take(results, sem)
+
+        else:
+            take(results, sem)
+
+    @pl.when(s == 0)
+    def _():
+        for i in range(4):
+            core, xc = i // 2, 2 * half + i % 2
+            deliver(scores.at[micro], core, xc, y, send_g.at[i], recv_p.at[micro], core == 0)
+
+    @pl.when(s == 1)
+    def _():
+        for k in range(3):
+            index = 2 * y + half - k + 2 * NY
+            for i in range(4):
+                core, xc, yc = i // 2, 2 * (index % 2) + i % 2, (index // 2) % NY
+                deliver(
+                    blocks.at[micro, k], core, xc, yc, send_g.at[4 * k + i], recv_g.at[micro, k], k < 2 and core == 1
+                )
+
+    def outgoing(line):
+        return jnp.where(half == 0, line[:, 0:ROWS], line[:, ROWS : 2 * ROWS])
+
+    for m in range(2):
+        take(scores.at[m], recv_p.at[m])
+        for k in range(3):
+            take(blocks.at[m, k], recv_g.at[m, k])
+        decay, through = carries[m]
+        third = blocks[m, 2, 0:1, 0:1] + LAMBDA_GAE * blocks[m, 2, 3:4, 0:1]
+        following = blocks[m, 1, 3:4, 0:1] + through * third
+        carry = blocks[m, 1, 0:1, 0:1] + LAMBDA_GAE * following
+        value = chain(blocks[m, 0, 0:3])
+        advantage = chain(blocks[m, 0, 3:6]) + decay * carry
+        out[m : m + 1, :] = outgoing(chain(scores[m, 0:3]))
+        out[2 + m : 3 + m, :] = outgoing(advantage)
+        out[4 + m : 5 + m, :] = outgoing(advantage + value)
+
     take(terms, send_t)
 
     @pl.when(s == 0)

time: 77.6 us -> 77.5 us (level)
  no operation moved by 1% of the time
where the time goes in v5:
time: 77.5 us; the launch traced here: 77.3 us
  Pallas kernels  76.7 us (99%)
    pallas_call x1, Pallas kernels, on_device(): pl.pallas_call(section_kernel, out_shape=jax.ShapeDtypeStruct((8, ROWS),...  75.4 us

profile of v5, /device:TPU:1, one launch (start us, length us, event | category | flops | bytes accessed | tf_op | source)
XLA Modules:
  0.0 77.3 jit_solution(14417109200839036124)
XLA Ops:
  0.6 75.4 %section.1.lines = f32[8,144]{1,0:T(8,128)} custom-call(bf16[2,144,8192]{2,1,0:T(8,128)(2,1)} %hid.1, f32[1,8192]{1,0:T(1,128)} %gain_hbm.1, bf16[256,512]{1,0:T(8,128)(2,1)} %bitcast.3, bf16[512,128]{1,0:T(8,128)(2,1)} %bitcast.4, f32[1,512]{1,0:T(1,128)} %bitcast.5, f32[2,512]{1,0:T(2,128)} %critic_hbm.1, s32[2,64]{1,0:T(2,128)} %lengths_hbm.1), custom_call_target="tpu_custom_call" | custom-call | tf_op jit(solution)/shard_map/section/pallas_call | solution.py:540
  76.0 1.3 %split.1 = (f32[2,144]{1,0:T(2,128)}, f32[2,144]{1,0:T(2,128)}, f32[2,144]{1,0:T(2,128)}) custom-call(f32[8,144]{1,0:T(8,128)} %section.1.lines), custom_call_target="tpu_custom_call" | custom-call | tf_op jit(solution)/shard_map/split/pallas_call | solution.py:589
